TPU v7x, 512 devices: a whole 4x8x8 slice. The times are simulated.
512 devices in a mesh: dp: 2 (over x_hi), tm: 16 (over z, x_lo), space: 16 (over y, core).
Axes of the slice: x: 4 (x_hi: 2, x_lo: 2; x = x_hi * 2 + x_lo), y: 8, z: 8, core: 2. Of those that a mesh axis runs over, the one named last changes fastest.
Arguments:
- queries: bfloat16 [4, 16, 32, 32, 1152], P('dp', 'tm', 'space'), may hold values from -6 to 6
- key_states: bfloat16 [4, 16, 32, 32, 1152], P('dp', 'tm', 'space'), may hold values from -6 to 6
- value_states: bfloat16 [4, 16, 32, 32, 1152], P('dp', 'tm', 'space'), may hold values from -6 to 6
- grad_out: bfloat16 [4, 16, 32, 32, 1152], P('dp', 'tm', 'space'), may hold values from -3 to 3
- attn_out: bfloat16 [4, 16, 32, 32, 1152], P('dp', 'tm', 'space'), may hold values from -6 to 6
- w_out: bfloat16 [1152, 1152], P('tm'), may hold values from -0.1875 to 0.1875
Outputs:
- grad_queries: bfloat16 [4, 16, 32, 32, 1152], P('dp', 'tm', 'space')
- grad_keys: bfloat16 [4, 16, 32, 32, 1152], P('dp', 'tm', 'space')
- grad_values: bfloat16 [4, 16, 32, 32, 1152], P('dp', 'tm', 'space')
- grad_w_out: float32 [1152, 1152], P('tm')
All inputs are finite; a program needn't handle non-finite values.
Results may differ from a plain program's by a relative error of at most 0.02.
Values may be sent and summed in bfloat16 or wider, within the bound.
No kernel may reach another device: no remote copies, remote signals or barrier semaphores. Data moves between devices by JAX's collectives and lax.ppermute only.
A program may use at most 64 MiB of HBM per device.

v0:
```python
import math

import jax
import jax.numpy as jnp
from jax import lax
from jax.sharding import PartitionSpec as P

D = 1152
HEADS = 16
HD = 72


def as_sent(array):
    return jax.tree.map(lambda a: a.astype(jnp.bfloat16) if a.dtype == jnp.float32 else a, array)


def frame_backward(q_rows, k_rows, v_rows, d_rows):
    scale_factor = 1.0 / math.sqrt(q_rows.shape[-1])
    scores = (
        jnp.einsum("xhd,yhd->hxy", q_rows, k_rows, preferred_element_type=jnp.float32)
        * scale_factor
    )
    highest = jnp.max(scores, axis=-1, keepdims=True)
    weights = jnp.exp(scores - highest)
    probabilities = weights / jnp.sum(weights, axis=-1, keepdims=True)
    rounded = probabilities.astype(jnp.bfloat16)
    grad_v = jnp.einsum("hxy,xhd->yhd", rounded, d_rows, preferred_element_type=jnp.float32).astype(
        jnp.bfloat16
    )
    grad_p = jnp.einsum("xhd,yhd->hxy", d_rows, v_rows, preferred_element_type=jnp.float32)
    row_terms = jnp.sum(probabilities * grad_p, axis=-1, keepdims=True)
    grad_s = (probabilities * (grad_p - row_terms)).astype(jnp.bfloat16)
    grad_q = (
        jnp.einsum("hxy,yhd->xhd", grad_s, k_rows, preferred_element_type=jnp.float32)
        * scale_factor
    ).astype(jnp.bfloat16)
    grad_k = (
        jnp.einsum("hxy,xhd->yhd", grad_s, q_rows, preferred_element_type=jnp.float32)
        * scale_factor
    ).astype(jnp.bfloat16)
    return (grad_q, grad_k, grad_v)


def per_frame(bundle):
    return frame_backward(bundle[0], bundle[1], bundle[2], bundle[3])


def attend(pieces):
    layout = pieces[0].shape
    amount = layout[0] * layout[1]
    merged = tuple(
        (member.reshape(amount, layout[2] * layout[3], layout[4], layout[5]) for member in pieces)
    )
    results = lax.map(per_frame, merged)
    restored = tuple((member.reshape(layout) for member in results))
    return jax.tree.map(
        lambda part, own: part.astype(own.dtype),
        lax.all_to_all(as_sent(restored), "space", split_axis=2, concat_axis=4, tiled=True),
        restored,
    )


def shards(queries, key_states, value_states, grad_out, attn_out, w_out):
    local_shape = queries.shape
    head_shape = local_shape[:4] + (HEADS, HD)
    flat_grad = grad_out.reshape(-1, D)
    head_grad = (
        jnp.einsum(
            "td,cd->tc",
            flat_grad,
            lax.all_gather(w_out, "tm", axis=0, tiled=True),
            preferred_element_type=jnp.float32,
        )
        .astype(jnp.bfloat16)
        .reshape(head_shape)
    )
    grad_parts = attend(
        (
            lax.all_to_all(
                queries.reshape(head_shape), "space", split_axis=4, concat_axis=2, tiled=True
            ),
            lax.all_to_all(
                key_states.reshape(head_shape), "space", split_axis=4, concat_axis=2, tiled=True
            ),
            lax.all_to_all(
                value_states.reshape(head_shape), "space", split_axis=4, concat_axis=2, tiled=True
            ),
            lax.all_to_all(head_grad, "space", split_axis=4, concat_axis=2, tiled=True),
        )
    )
    flat_attn = attn_out.reshape(-1, D)
    shard_sum = lax.psum_scatter(
        jnp.einsum("tc,td->cd", flat_attn, flat_grad, preferred_element_type=jnp.float32).astype(
            jnp.bfloat16
        ),
        "tm",
        scatter_dimension=0,
        tiled=True,
    ).astype(jnp.float32)
    grad_w_out = lax.psum(shard_sum, ("dp", "space"))
    return (
        grad_parts[0].reshape(local_shape),
        grad_parts[1].reshape(local_shape),
        grad_parts[2].reshape(local_shape),
        grad_w_out,
    )


def solution(mesh):
    return jax.shard_map(
        shards,
        mesh=mesh,
        in_specs=(
            P("dp", "tm", "space", None, None),
            P("dp", "tm", "space", None, None),
            P("dp", "tm", "space", None, None),
            P("dp", "tm", "space", None, None),
            P("dp", "tm", "space", None, None),
            P("tm", None),
        ),
        out_specs=(
            P("dp", "tm", "space", None, None),
            P("dp", "tm", "space", None, None),
            P("dp", "tm", "space", None, None),
            P("tm", None),
        ),
        check_vma=False,
    )
```

profile of v0, /device:TPU:1, one launch (start us, length us, event | category | flops | bytes accessed | tf_op | source)
XLA Modules:
  0.0 331.0 jit_solution(7353083505266189792)
XLA Ops:
  7.2 0.7 all-gather.2.cloned.1.call-update
  7.9 1.9 reshape.131
  9.8 0.9 copy.66
  10.8 10.2 %all-to-all-start = ((bf16[2,1,2,32,16,72]{5,3,2,0,1,4:T(8,128)(2,1)}), bf16[2,1,2,32,16,72]{5,3,2,0,1,4:T(8,128)(2,1)S(1)}, u32[]{:S(2)}, u32[]{:S(2)}) async-start(bf16[2,1,2,32,16,72]{5,3,2,0,1,4:T(8,128)(2,1)} %copy.66), calls=%async_computation | async-start | bytes 1048576 | tf_op jit(solution)/shard_map/all_to_all | solution.py:82
  21.0 1.9 reshape.133
  22.9 0.9 copy.68
  23.9 14.5 %all-to-all-done = bf16[2,1,2,32,16,72]{5,3,2,0,1,4:T(8,128)(2,1)S(1)} async-done(((bf16[2,1,2,32,16,72]{5,3,2,0,1,4:T(8,128)(2,1)}), bf16[2,1,2,32,16,72]{5,3,2,0,1,4:T(8,128)(2,1)S(1)}, u32[]{:S(2)}, u32[]{:S(2)}) %all-to-all-start) | async-done | bytes 294944 | tf_op jit(solution)/shard_map/all_to_all | solution.py:82
  38.4 3.5 %all-to-all-start.1 = ((bf16[2,1,2,32,16,72]{5,3,2,0,1,4:T(8,128)(2,1)}), bf16[2,1,2,32,16,72]{5,3,2,0,1,4:T(8,128)(2,1)S(1)}, u32[]{:S(2)}, u32[]{:S(2)}) async-start(bf16[2,1,2,32,16,72]{5,3,2,0,1,4:T(8,128)(2,1)} %copy.68), calls=%async_computation.1 | async-start | bytes 1048576 | tf_op jit(solution)/shard_map/all_to_all | solution.py:79
  41.8 0.9 reshape.138
  42.8 0.9 copy.72
  43.7 14.8 %all-to-all-done.1 = bf16[2,1,2,32,16,72]{5,3,2,0,1,4:T(8,128)(2,1)S(1)} async-done(((bf16[2,1,2,32,16,72]{5,3,2,0,1,4:T(8,128)(2,1)}), bf16[2,1,2,32,16,72]{5,3,2,0,1,4:T(8,128)(2,1)S(1)}, u32[]{:S(2)}, u32[]{:S(2)}) %all-to-all-start.1) | async-done | bytes 294944 | tf_op jit(solution)/shard_map/all_to_all | solution.py:79
  58.5 3.5 %all-to-all-start.3 = ((bf16[2,1,2,32,16,72]{5,3,2,0,1,4:T(8,128)(2,1)}), bf16[2,1,2,32,16,72]{5,3,2,0,1,4:T(8,128)(2,1)S(1)}, u32[]{:S(2)}, u32[]{:S(2)}) async-start(bf16[2,1,2,32,16,72]{5,3,2,0,1,4:T(8,128)(2,1)} %copy.72), calls=%async_computation.3 | async-start | bytes 1048576 | tf_op jit(solution)/shard_map/all_to_all | solution.py:85
  62.0 26.2 %all-gather.2.cloned.1.call-done = bf16[1152,1152]{1,0:T(8,128)(2,1)} async-done(((bf16[72,1152]{1,0:T(8,128)(2,1)}), bf16[1152,1152]{1,0:T(8,128)(2,1)}) %all-gather.2.cloned.1.call-update) | async-done | bytes 2654224 | tf_op jit(solution)/shard_map/all_gather | solution.py:71
  88.2 2.7 convolution_convert_fusion
  90.8 0.9 reshape.136
  91.8 0.9 copy.70
  92.7 15.4 %all-to-all-start.2 = ((bf16[2,1,2,32,16,72]{5,3,2,0,1,4:T(8,128)(2,1)}), bf16[2,1,2,32,16,72]{5,3,2,0,1,4:T(8,128)(2,1)S(1)}, u32[]{:S(2)}, u32[]{:S(2)}) async-start(bf16[2,1,2,32,16,72]{5,3,2,0,1,4:T(8,128)(2,1)} %copy.70), calls=%async_computation.2 | async-start | bytes 1048576 | tf_op jit(solution)/shard_map/all_to_all | solution.py:88
  108.4 2.4 fusion.41
  111.6 13.9 %all-to-all-done.2 = bf16[2,1,2,32,16,72]{5,3,2,0,1,4:T(8,128)(2,1)S(1)} async-done(((bf16[2,1,2,32,16,72]{5,3,2,0,1,4:T(8,128)(2,1)}), bf16[2,1,2,32,16,72]{5,3,2,0,1,4:T(8,128)(2,1)S(1)}, u32[]{:S(2)}, u32[]{:S(2)}) %all-to-all-start.2) | async-done | bytes 294944 | tf_op jit(solution)/shard_map/all_to_all | solution.py:88
  125.7 12.3 %while.14 = (s32[]{:T(128)}, bf16[2,1024,1,72]{1,3,2,0:T(8,128)(2,1)S(1)}, bf16[2,1024,1,72]{1,3,2,0:T(8,128)(2,1)S(1)}, bf16[2,1024,1,72]{1,3,2,0:T(8,128)(2,1)...) while((s32[]{:T(128)}, ...), condition=%wide.region_4.5_spmd, body=%wide.region_0.4_spmd.sunk | while | flops 776311808 | bytes 39535764 | solution.py:54
  125.7 0.8 multiply_reduce_fusion.4
  126.5 0.7 fusion.64
  127.3 1.0 fusion.67
  128.3 1.2 multiply_reduce_fusion.5
  129.5 1.2 multiply_convert_fusion.2
  130.6 0.8 fusion.66
  131.4 0.5 fusion.65
  131.9 0.8 multiply_reduce_fusion.4
  132.7 0.7 fusion.64
  133.4 1.0 fusion.67
  134.4 1.2 multiply_reduce_fusion.5
  135.6 1.2 multiply_convert_fusion.2
  136.8 0.8 fusion.66
  137.6 0.5 fusion.65
  138.4 0.9 copy.79
  139.2 3.5 %all-to-all-start.4 = ((bf16[2,1,32,32,1,72]{5,3,0,4,1,2:T(8,128)(2,1)}), bf16[2,1,32,32,1,72]{5,3,0,4,1,2:T(8,128)(2,1)S(1)}, u32[]{:S(2)}, u32[]{:S(2)}) async-start(bf16[2,1,32,32,1,72]{5,3,0,4,1,2:T(8,128)(2,1)} %copy.79), calls=%async_computation.4 | async-start | bytes 1048576 | tf_op jit(solution)/shard_map/all_to_all | solution.py:58
  143.0 0.9 copy.83
  143.9 15.6 %all-to-all-done.4 = bf16[2,1,32,32,1,72]{5,3,0,4,1,2:T(8,128)(2,1)S(1)} async-done(((bf16[2,1,32,32,1,72]{5,3,0,4,1,2:T(8,128)(2,1)}), bf16[2,1,32,32,1,72]{5,3,0,4,1,2:T(8,128)(2,1)S(1)}, u32[]{:S(2)}, u32[]{:S(2)}) %all-to-all-start.4) | async-done | bytes 294944 | tf_op jit(solution)/shard_map/all_to_all | solution.py:58
  159.4 3.5 %all-to-all-start.5 = ((bf16[2,1,32,32,1,72]{5,3,0,4,1,2:T(8,128)(2,1)}), bf16[2,1,32,32,1,72]{5,3,0,4,1,2:T(8,128)(2,1)S(1)}, u32[]{:S(2)}, u32[]{:S(2)}) async-start(bf16[2,1,32,32,1,72]{5,3,0,4,1,2:T(8,128)(2,1)} %copy.83), calls=%async_computation.5 | async-start | bytes 1048576 | tf_op jit(solution)/shard_map/all_to_all | solution.py:58
  163.2 0.9 copy.87
  164.1 15.6 %all-to-all-done.5 = bf16[2,1,32,32,1,72]{5,3,0,4,1,2:T(8,128)(2,1)S(1)} async-done(((bf16[2,1,32,32,1,72]{5,3,0,4,1,2:T(8,128)(2,1)}), bf16[2,1,32,32,1,72]{5,3,0,4,1,2:T(8,128)(2,1)S(1)}, u32[]{:S(2)}, u32[]{:S(2)}) %all-to-all-start.5) | async-done | bytes 294944 | tf_op jit(solution)/shard_map/all_to_all | solution.py:58
  179.6 3.5 %all-to-all-start.6 = ((bf16[2,1,32,32,1,72]{5,3,0,4,1,2:T(8,128)(2,1)}), bf16[2,1,32,32,1,72]{5,3,0,4,1,2:T(8,128)(2,1)S(1)}, u32[]{:S(2)}, u32[]{:S(2)}) async-start(bf16[2,1,32,32,1,72]{5,3,0,4,1,2:T(8,128)(2,1)} %copy.87), calls=%async_computation.6 | async-start | bytes 1048576 | tf_op jit(solution)/shard_map/all_to_all | solution.py:58
  183.2 136.1 %all-reduce.2 = f32[72,1152]{1,0:T(8,128)} all-reduce(bf16[72,1152]{1,0:T(8,128)(2,1)} %reduce-scatter.5.cloned.1.call-done), channel_id=1, replica_groups=mesh['dp'=2,'tm'=16,'space'=16] {'dp','space'}, use_global_device_ids=true, to_apply=%region_6.7 | all-reduce | flops 82944 | bytes 497664 | tf_op jit(solution)/shard_map/psum | solution.py:100
  319.3 0.3 copy.81
  319.6 1.2 reshape.141
  320.9 0.3 copy.85
  321.2 1.2 reshape.143
  322.9 1.2 reshape.145
  (40 shorter events, 2.5 us)
Async XLA Ops:
  7.2 81.0 %copy-start = (bf16[2,1,2,32,1152]{4,3,2,1,0:T(8,128)(2,1)S(1)}, bf16[2,1,2,32,1152]{4,3,2,1,0:T(8,128)(2,1)}, u32[]{:S(2)}) copy-start(bf16[2,1,2,32,1152]{4,3,2,1,0:T(8,128)(2,1)} %param.11) | copy-start | bytes 884740
  7.2 34.7 %copy-start.1 = (bf16[2,1,2,32,1152]{4,3,2,1,0:T(8,128)(2,1)S(1)}, bf16[2,1,2,32,1152]{4,3,2,1,0:T(8,128)(2,1)}, u32[]{:S(2)}) copy-start(bf16[2,1,2,32,1152]{4,3,2,1,0:T(8,128)(2,1)} %param.10) | copy-start | bytes 884740
  7.2 81.0 %all-gather.2.cloned.1.call-start = ((), (), s32[]{:S(2)}) async-start(), calls=%async_computation.8 | async-start | bytes 2820096 | tf_op jit(solution)/shard_map/all_gather | solution.py:71
  10.8 27.6 %all-to-all-start = ((bf16[2,1,2,32,16,72]{5,3,2,0,1,4:T(8,128)(2,1)}), bf16[2,1,2,32,16,72]{5,3,2,0,1,4:T(8,128)(2,1)S(1)}, u32[]{:S(2)}, u32[]{:S(2)}) async-start(bf16[2,1,2,32,16,72]{5,3,2,0,1,4:T(8,128)(2,1)} %copy.66), calls=%async_computation | async-start | bytes 1048576 | tf_op jit(solution)/shard_map/all_to_all | solution.py:82
  38.4 20.2 %all-to-all-start.1 = ((bf16[2,1,2,32,16,72]{5,3,2,0,1,4:T(8,128)(2,1)}), bf16[2,1,2,32,16,72]{5,3,2,0,1,4:T(8,128)(2,1)S(1)}, u32[]{:S(2)}, u32[]{:S(2)}) async-start(bf16[2,1,2,32,16,72]{5,3,2,0,1,4:T(8,128)(2,1)} %copy.68), calls=%async_computation.1 | async-start | bytes 1048576 | tf_op jit(solution)/shard_map/all_to_all | solution.py:79
  42.8 65.6 %copy-start.5 = (bf16[2,1,2,32,1152]{4,3,2,1,0:T(8,128)(2,1)S(1)}, bf16[2,1,2,32,1152]{4,3,2,1,0:T(8,128)(2,1)}, u32[]{:S(2)}) copy-start(bf16[2,1,2,32,1152]{4,3,2,1,0:T(8,128)(2,1)} %param.12) | copy-start | bytes 884740
  58.5 34.2 %all-to-all-start.3 = ((bf16[2,1,2,32,16,72]{5,3,2,0,1,4:T(8,128)(2,1)}), bf16[2,1,2,32,16,72]{5,3,2,0,1,4:T(8,128)(2,1)S(1)}, u32[]{:S(2)}, u32[]{:S(2)}) async-start(bf16[2,1,2,32,16,72]{5,3,2,0,1,4:T(8,128)(2,1)} %copy.72), calls=%async_computation.3 | async-start | bytes 1048576 | tf_op jit(solution)/shard_map/all_to_all | solution.py:85
  92.7 32.7 %all-to-all-start.2 = ((bf16[2,1,2,32,16,72]{5,3,2,0,1,4:T(8,128)(2,1)}), bf16[2,1,2,32,16,72]{5,3,2,0,1,4:T(8,128)(2,1)S(1)}, u32[]{:S(2)}, u32[]{:S(2)}) async-start(bf16[2,1,2,32,16,72]{5,3,2,0,1,4:T(8,128)(2,1)} %copy.70), calls=%async_computation.2 | async-start | bytes 1048576 | tf_op jit(solution)/shard_map/all_to_all | solution.py:88
  108.2 75.0 %reduce-scatter.5.cloned.1.call-start = ((), (), s32[]{:S(2)}) async-start(), calls=%async_computation.9 | async-start | bytes 2820096
  125.7 1.5 copy-start.2
  128.2 1.2 copy-start.3
  131.9 1.5 copy-start.2
  134.4 1.2 copy-start.3
  138.1 24.8 %copy-start.4 = (bf16[2,1024,1,72]{1,3,2,0:T(8,128)(2,1)S(1)}, bf16[2,1024,1,72]{1,3,2,0:T(8,128)(2,1)}, u32[]{:S(2)}) copy-start(bf16[2,1024,1,72]{1,3,2,0:T(8,128)(2,1)} %get-tuple-element.50) | copy-start | bytes 884740
  139.2 20.2 %all-to-all-start.4 = ((bf16[2,1,32,32,1,72]{5,3,0,4,1,2:T(8,128)(2,1)}), bf16[2,1,32,32,1,72]{5,3,0,4,1,2:T(8,128)(2,1)S(1)}, u32[]{:S(2)}, u32[]{:S(2)}) async-start(bf16[2,1,32,32,1,72]{5,3,0,4,1,2:T(8,128)(2,1)} %copy.79), calls=%async_computation.4 | async-start | bytes 1048576 | tf_op jit(solution)/shard_map/all_to_all | solution.py:58
  159.4 20.2 %all-to-all-start.5 = ((bf16[2,1,32,32,1,72]{5,3,0,4,1,2:T(8,128)(2,1)}), bf16[2,1,32,32,1,72]{5,3,0,4,1,2:T(8,128)(2,1)S(1)}, u32[]{:S(2)}, u32[]{:S(2)}) async-start(bf16[2,1,32,32,1,72]{5,3,0,4,1,2:T(8,128)(2,1)} %copy.83), calls=%async_computation.5 | async-start | bytes 1048576 | tf_op jit(solution)/shard_map/all_to_all | solution.py:58
  179.6 142.8 %all-to-all-start.6 = ((bf16[2,1,32,32,1,72]{5,3,0,4,1,2:T(8,128)(2,1)}), bf16[2,1,32,32,1,72]{5,3,0,4,1,2:T(8,128)(2,1)S(1)}, u32[]{:S(2)}, u32[]{:S(2)}) async-start(bf16[2,1,32,32,1,72]{5,3,0,4,1,2:T(8,128)(2,1)} %copy.87), calls=%async_computation.6 | async-start | bytes 1048576 | tf_op jit(solution)/shard_map/all_to_all | solution.py:58
Sparse Core Ops, SparseCore 0:
  10.1 78.0 all-gather.1
  111.9 68.5 reduce-scatter.4
where the time goes:
time: 336 us; the launch traced here: 331 us
  blocking collectives  136 us (40%)
  waiting for transfers between devices  101 us (30%)
  starting transfers between devices  43.2 us (13%)
  local copies, waits for them, and re-layouts  18.7 us (6%)
  between operations  14.3 us (4%)
  matrix products  13.5 us (4%)
  other arithmetic  3.77 us (1%)
    psum x1, blocking collectives, shards(): grad_w_out = lax.psum(shard_sum, ('dp', 'space'))  136 us
    all_to_all x3, waiting for transfers between devices, attend(): lax.all_to_all(as_sent(restored), 'space', split_axis=2, concat_axis=4, t...  31.1 us
    all_gather x1, waiting for transfers between devices, shards(): lax.all_gather(w_out, 'tm', axis=0, tiled=True)  26.2 us
    all_to_all x1, starting transfers between devices, shards(): lax.all_to_all(head_grad, 'space', split_axis=4, concat_axis=2, tiled=True)  15.4 us
    all_to_all x1, waiting for transfers between devices, shards(): lax.all_to_all(queries.reshape(head_shape), 'space', split_axis=4, concat...  14.8 us
    all_to_all x1, waiting for transfers between devices, shards(): lax.all_to_all(key_states.reshape(head_shape), 'space', split_axis=4, con...  14.5 us
    all_to_all x1, waiting for transfers between devices, shards(): lax.all_to_all(head_grad, 'space', split_axis=4, concat_axis=2, tiled=True)  13.9 us
    all_to_all x3, starting transfers between devices, attend(): lax.all_to_all(as_sent(restored), 'space', split_axis=2, concat_axis=4, t...  10.4 us
  transfers between devices with their start and end apart: 9, of which 6 were waited for; matrix products, arithmetic and copies ran while one was open for 10% of the time, Pallas kernels for 0%

commit v1 on v0

v1 whole, which is shorter than its diff:
```python
import math

import jax
import jax.numpy as jnp
from jax import lax
from jax.experimental import pallas as pl
from jax.experimental.pallas import tpu as pltpu
from jax.sharding import Mesh
from jax.sharding import PartitionSpec as P

D = 1152
HEADS = 16
HD = 72
TOKENS = 128
FRAME = 1024
HALF = 40
PIECE = 48
QUERIES = 256
SCALE = 1.0 / math.sqrt(HD)
LOG2E = math.log2(math.e)
BF16 = jnp.bfloat16
F32 = jnp.float32
SPACE = ("y", "core")


def dot(a, b, dim_a, dim_b):
    return lax.dot_general(a, b, (((dim_a,), (dim_b,)), ((), ())), preferred_element_type=F32)


def pack_kernel(q_ref, k_ref, v_ref, out_ref):
    for j, ref in enumerate((q_ref, k_ref, v_ref)):
        turned = ref[...].astype(F32).T
        for h in range(HEADS):
            out_ref[h, j] = turned[HD * h : HD * h + HD].astype(BF16)


def pack(q, k, v):
    return pl.pallas_call(
        pack_kernel,
        out_shape=jax.ShapeDtypeStruct((HEADS, 3, HD, TOKENS), BF16),
        compiler_params=pltpu.CompilerParams(vmem_limit_bytes=16 * 2**20),
        cost_estimate=pl.CostEstimate(flops=0, bytes_accessed=2 * 2**20, transcendentals=0),
    )(q, k, v)


def unpack_kernel(x_ref, q_ref, k_ref, v_ref):
    for j, ref in enumerate((q_ref, k_ref, v_ref)):
        whole = jnp.concatenate([x_ref[h, j].astype(F32) for h in range(HEADS)], axis=0)
        ref[...] = whole.T.astype(BF16)


def unpack(x):
    out = jax.ShapeDtypeStruct((TOKENS, D), BF16)
    return pl.pallas_call(
        unpack_kernel,
        out_shape=(out, out, out),
        compiler_params=pltpu.CompilerParams(vmem_limit_bytes=16 * 2**20),
        cost_estimate=pl.CostEstimate(flops=0, bytes_accessed=2 * 2**20, transcendentals=0),
    )(x)


def pair_videos(first, second):
    low = lax.broadcasted_iota(jnp.int32, first.shape, 1) < 64
    return (
        jnp.where(low, first, pltpu.roll(second, 64, 1)),
        jnp.where(low, pltpu.roll(first, 64, 1), second),
    )


def attention_kernel(qkv_ref, g_ref, out_ref, held):
    for i in range(HEADS // 2):
        lanes = slice(TOKENS * i, TOKENS * (i + 1))
        for j in range(3):
            pair = pair_videos(qkv_ref[2 * i, j].astype(F32), qkv_ref[2 * i + 1, j].astype(F32))
            held[0, j, :, lanes] = pair[0].astype(BF16)
            held[1, j, :, lanes] = pair[1].astype(BF16)
        upper, lower = g_ref[2 * i].astype(F32), g_ref[2 * i + 1].astype(F32)
        g = jnp.concatenate([upper, lower[2 * HALF - HD :]], axis=0)
        pair = pair_videos(g[:, :TOKENS], g[:, TOKENS:])
        held[0, 3, :, lanes] = pair[0].astype(BF16)
        held[1, 3, :, lanes] = pair[1].astype(BF16)
    results = []
    for video in range(2):
        k, v = held[video, 1], held[video, 2]
        grad_q = []
        grad_k = jnp.zeros((HD, FRAME), F32)
        grad_v = jnp.zeros((HD, FRAME), F32)
        for step in range(FRAME // QUERIES):
            lanes = slice(QUERIES * step, QUERIES * (step + 1))
            q, g = held[video, 0, :, lanes], held[video, 3, :, lanes]
            scores = dot(q, k, 0, 0)
            highest = jnp.max(scores, axis=1, keepdims=True)
            weights = jnp.exp2((scores - highest) * (SCALE * LOG2E))
            probabilities = weights * (1.0 / jnp.sum(weights, axis=1, keepdims=True))
            grad_p = dot(g, v, 0, 0)
            row_terms = jnp.sum(probabilities * grad_p, axis=1, keepdims=True)
            grad_s = (probabilities * (grad_p - row_terms)).astype(BF16)
            grad_v = grad_v + dot(g, probabilities.astype(BF16), 1, 0)
            grad_k = grad_k + dot(q, grad_s, 1, 0)
            grad_q.append(dot(k, grad_s, 1, 1))
        results.append((jnp.concatenate(grad_q, axis=1) * SCALE, grad_k * SCALE, grad_v))
    for i in range(HEADS // 2):
        lanes = slice(TOKENS * i, TOKENS * (i + 1))
        for j in range(3):
            pair = pair_videos(results[0][j][:, lanes], results[1][j][:, lanes])
            out_ref[2 * i, j] = pair[0].astype(BF16)
            out_ref[2 * i + 1, j] = pair[1].astype(BF16)


def attention(qkv, g):
    return pl.pallas_call(
        attention_kernel,
        out_shape=jax.ShapeDtypeStruct((HEADS, 3, HD, TOKENS), BF16),
        scratch_shapes=[pltpu.VMEM((2, 4, HD, FRAME), BF16)],
        compiler_params=pltpu.CompilerParams(vmem_limit_bytes=48 * 2**20),
        cost_estimate=pl.CostEstimate(
            flops=2 * 2 * 5 * FRAME * FRAME * 256,
            bytes_accessed=3 * 2**20,
            transcendentals=2 * FRAME * FRAME,
        ),
    )(qkv, g)


def exchange(x, axis):
    return lax.ppermute(x, axis, [(0, 1), (1, 0)])


def all_to_all(x, axis):
    return lax.all_to_all(x, axis, split_axis=0, concat_axis=0, tiled=True)


def interleave_kernel(after_ref, even_ref, odd_ref, out_ref):
    for i in range(HEADS // 2):
        out_ref[2 * i] = even_ref[i]
        out_ref[2 * i + 1] = odd_ref[i]


def interleave_after(after, even, odd):
    vmem = pl.BlockSpec(memory_space=pltpu.VMEM)
    return pl.pallas_call(
        interleave_kernel,
        out_shape=jax.ShapeDtypeStruct((HEADS, HALF, 2 * TOKENS), BF16),
        in_specs=[pl.BlockSpec(memory_space=pl.ANY), vmem, vmem],
        compiler_params=pltpu.CompilerParams(vmem_limit_bytes=8 * 2**20),
        cost_estimate=pl.CostEstimate(flops=0, bytes_accessed=2**20, transcendentals=0),
    )(after, even, odd)


def head_cotangents(grad_out, w_rows, after):
    parity = lax.axis_index("xl")
    gathered = lax.all_gather(w_rows, "z", axis=0, tiled=True)
    tokens = lax.all_gather(grad_out, ("xl", "core"), axis=0, tiled=True)
    both = dot(gathered, tokens, 1, 1).astype(BF16)
    own = lax.dynamic_slice_in_dim(both, 2 * TOKENS * parity, 2 * TOKENS, axis=1)
    other = lax.dynamic_slice_in_dim(both, 2 * TOKENS * (1 - parity), 2 * TOKENS, axis=1)
    arrived = exchange(other, "xl").reshape(HEADS // 2, HALF, 2 * TOKENS)
    own = own.reshape(HEADS // 2, HALF, 2 * TOKENS)
    even = jnp.where(parity == 0, own, arrived)
    odd = jnp.where(parity == 0, arrived, own)
    return interleave_after(after, even, odd)


def along_x(x, flip_dp, flip_xl):
    pairs = [(2 * a + b, 2 * (a ^ flip_dp) + (b ^ flip_xl)) for a in (0, 1) for b in (0, 1)]
    return lax.ppermute(x, ("dp", "xl"), pairs)


def add_kernel(after_ref, a_ref, b_ref, c_ref, d_ref, out_ref):
    total = a_ref[...].astype(F32) + b_ref[...].astype(F32)
    total = total + c_ref[...].astype(F32) + d_ref[...].astype(F32)
    out_ref[...] = total.astype(BF16)


def add_after(after, parts):
    vmem = pl.BlockSpec(memory_space=pltpu.VMEM)
    return pl.pallas_call(
        add_kernel,
        out_shape=jax.ShapeDtypeStruct(parts[0].shape, BF16),
        in_specs=[pl.BlockSpec(memory_space=pl.ANY)] + [vmem] * 4,
        compiler_params=pltpu.CompilerParams(vmem_limit_bytes=8 * 2**20),
        cost_estimate=pl.CostEstimate(flops=0, bytes_accessed=2**20, transcendentals=0),
    )(after, *parts)


def sum_along_x(rows, after):
    parity = lax.axis_index("xl")
    own = lax.dynamic_slice_in_dim(rows, HD * parity, HD, axis=0)
    other = lax.dynamic_slice_in_dim(rows, HD * (1 - parity), HD, axis=0)
    parts = (own, along_x(other, 0, 1), along_x(own, 1, 0), along_x(other, 1, 1))
    return add_after(after, parts)


def to_pieces(x):
    tiles = x.reshape(9, 8, 9, 128).transpose(0, 2, 1, 3).reshape(81, 8, 128)
    return jnp.pad(tiles, ((0, 15), (0, 0), (0, 0))).reshape(HEADS, PIECE, 128)


def from_pieces(x):
    tiles = x.reshape(96, 8, 128)[:81].reshape(9, 9, 8, 128)
    return tiles.transpose(0, 2, 1, 3).reshape(HD, D)


def shards(queries, key_states, value_states, grad_out, attn_out, w_out):
    local_shape = queries.shape
    q, k, v, grad_out, attn_out = (
        a.reshape(TOKENS, D) for a in (queries, key_states, value_states, grad_out, attn_out)
    )
    core = lax.axis_index("core")
    term = dot(attn_out, grad_out, 0, 0).astype(BF16)
    rows = lax.psum_scatter(term, "z", scatter_dimension=0, tiled=True)
    w_rows = lax.dynamic_slice_in_dim(w_out, (HD - HALF) * core, HALF, axis=0)
    packed, w_rows = lax.optimization_barrier((pack(q, k, v), w_rows))
    qkv = all_to_all(packed, SPACE)
    g = head_cotangents(grad_out, w_rows, qkv)
    g, rows = lax.optimization_barrier((g, rows))
    g = all_to_all(g, SPACE)
    pieces = all_to_all(to_pieces(sum_along_x(rows, g)), SPACE)
    piece = jnp.sum(pieces.astype(F32), axis=0, keepdims=True).astype(BF16)
    sent = jnp.concatenate(
        [
            attention(qkv, g).reshape(HEADS, 3 * HD, 128),
            jnp.broadcast_to(piece, (HEADS, PIECE, 128)),
        ],
        axis=1,
    )
    arrived = all_to_all(sent, SPACE)
    grads = unpack(arrived[:, : 3 * HD].reshape(HEADS, 3, HD, TOKENS))
    grad_w_out = from_pieces(arrived[:, 3 * HD :].astype(F32))
    return tuple(a.reshape(local_shape) for a in grads) + (grad_w_out,)


def solution(mesh):
    fine = Mesh(mesh.devices.reshape(2, 8, 2, 8, 2), ("dp", "z", "xl", "y", "core"))
    tokens = P("dp", ("z", "xl"), ("y", "core"), None, None)
    rows = P(("z", "xl"), None)
    return jax.shard_map(
        shards,
        mesh=fine,
        in_specs=(tokens,) * 5 + (rows,),
        out_specs=(tokens,) * 3 + (rows,),
        check_vma=False,
    )
```

time: 336 us -> 157 us (0.47); the launches traced: 331 us -> 156 us
  waiting for transfers between devices: 101 us -> 16 us
  blocking collectives: 136 us -> 64 us
  local copies, waits for them, and re-layouts: 18.7 us -> 3.14 us
  Pallas kernels: 0 us -> 11.2 us
  matrix products: 13.5 us -> 5.24 us
    psum x1 -> x0, blocking collectives: 136 us -> none  [shards(): grad_w_out = lax.psum(shard_sum, ('dp', 'space'))]
    all_to_all x7 -> x3, waiting for transfers between devices: 74.3 us -> 2.28 us  [all_to_all(): return lax.all_to_all(x, axis, split_axis=0, concat_axis=0, tiled=True)]
    all_to_all x0 -> x1, blocking collectives: none -> 34.4 us  [all_to_all(): return lax.all_to_all(x, axis, split_axis=0, concat_axis=0, tiled=True)]
    all_gather x0 -> x1, blocking collectives: none -> 29.6 us  [head_cotangents(): gathered = lax.all_gather(w_rows, 'z', axis=0, tiled=True)]
    all_gather x1, waiting for transfers between devices: 26.2 us -> 0.01 us  [head_cotangents(): tokens = lax.all_gather(grad_out, ('xl', 'core'), axis=0, tiled=True)]
    all_to_all x7 -> x3, starting transfers between devices: 43 us -> 27.2 us  [all_to_all(): return lax.all_to_all(x, axis, split_axis=0, concat_axis=0, tiled=True)]
    reshape x14 -> x0, local copies, waits for them, and re-layouts: 15.8 us -> none  [the longest x2 2.85 us: shards(): queries.reshape(head_shape)]
    ppermute x0 -> x4, starting transfers between devices: none -> 13 us  [the longest x3 9.61 us: along_x(): return lax.ppermute(x, ('dp', 'xl'), pairs)]
  transfers between devices with their start and end apart: 9 -> 9, of which waited for: 6 -> 5; matrix products, arithmetic and copies ran while one was open for 10% -> 4% of each run, Pallas kernels for 0% -> 6%
where the time goes in v1:
time: 157 us; the launch traced here: 156 us
  blocking collectives  64 us (41%)
  starting transfers between devices  40.2 us (26%)
  waiting for transfers between devices  16 us (10%)
  between operations  15.6 us (10%)
  Pallas kernels  11.2 us (7%)
  matrix products  5.24 us (3%)
  local copies, waits for them, and re-layouts  3.14 us (2%)
    all_to_all x1, blocking collectives, all_to_all(): return lax.all_to_all(x, axis, split_axis=0, concat_axis=0, tiled=True)  34.4 us
    all_gather x1, blocking collectives, head_cotangents(): gathered = lax.all_gather(w_rows, 'z', axis=0, tiled=True)  29.6 us
    all_to_all x3, starting transfers between devices, all_to_all(): return lax.all_to_all(x, axis, split_axis=0, concat_axis=0, tiled=True)  27.2 us
    ppermute x3, starting transfers between devices, along_x(): return lax.ppermute(x, ('dp', 'xl'), pairs)  9.61 us
    pallas_call x1, Pallas kernels, attention(): pl.pallas_call(attention_kernel, out_shape=jax.ShapeDtypeStruct((HEADS, 3...  8.04 us
    ppermute x3, waiting for transfers between devices, along_x(): return lax.ppermute(x, ('dp', 'xl'), pairs)  5.46 us
    dot_general x2, matrix products, dot(): lax.dot_general(a, b, (((dim_a,), (dim_b,)), ((), ())), preferred_element...  5.24 us
    reduce_scatter x1, waiting for transfers between devices, shards(): rows = lax.psum_scatter(term, 'z', scatter_dimension=0, tiled=True)  4.43 us
  transfers between devices with their start and end apart: 9, of which 5 were waited for; matrix products, arithmetic and copies ran while one was open for 4% of the time, Pallas kernels for 6%

profile of v1, /device:TPU:1, one launch (start us, length us, event | category | flops | bytes accessed | tf_op | source)
XLA Modules:
  0.0 156.3 jit_solution(1789108869267002107)
XLA Ops:
  8.0 0.0 copy-start
  8.0 0.0 all-gather.2.cloned.1.call-start
  8.1 0.7 all-gather.2.cloned.1.call-update
  8.7 0.0 reduce-scatter.2.cloned.1.call-start
  8.8 0.2 copy-done
  9.0 3.3 %fusion = bf16[1152,1152]{1,0:T(8,128)(2,1)} fusion(bf16[2,1,2,32,1152]{4,3,2,1,0:T(8,128)(2,1)} %param.9, bf16[2,1,2,32,1152]{4,3,2,1,0:T(8,128)(2,1)S(1)} %copy-done), kind=kOutput, calls=%fused_computation.1 | convolution fusion | flops 341065728 | bytes 3244032 | tf_op jit(solution)/shard_map/dot_general | solution.py:27
  12.3 0.0 copy-start.1
  12.3 0.0 copy-start.2
  12.3 0.0 copy-start.3
  12.3 0.0 reduce-scatter.2.cloned.1.call-update
  12.3 0.0 copy-start.4
  12.4 0.9 copy-done.1
  13.3 0.1 copy-done.2
  13.4 0.1 copy-done.3
  13.4 1.2 shard_map.93
  14.7 0.0 copy-done.4
  14.7 10.3 %all-to-all-start = ((bf16[16,3,72,128]{3,2,1,0:T(8,128)(2,1)}), bf16[16,3,72,128]{3,2,1,0:T(8,128)(2,1)S(1)}, u32[]{:S(2)}, u32[]{:S(2)}) async-start(bf16[16,3,72,128]{3,2,1,0:T(8,128)(2,1)} %shard_map.93), calls=%async_computation | async-start | bytes 1769472 | tf_op jit(solution)/shard_map/all_to_all | solution.py:129
  25.0 29.6 %all_gather.6 = bf16[320,1152]{1,0:T(8,128)(2,1)S(1)} all-gather(bf16[40,1152]{1,0:T(8,128)(2,1)S(1)} %constant_dynamic-slice_fusion.3), channel_id=1, replica_groups=mesh['dp'=2,'z'=8,'xl'=2,'y'=8,'core'=2] {'z'}, dimensions={0}, use_global_device_ids=true | all-gather | bytes 829440 | tf_op jit(solution)/shard_map/all_gather | solution.py:151
  54.6 0.0 all-gather.2.cloned.1.call-done
  54.6 1.9 %convolution_convert_fusion = bf16[320,512]{1,0:T(8,128)(2,1)S(1)} fusion(bf16[320,1152]{1,0:T(8,128)(2,1)S(1)} %all_gather.6, bf16[512,1152]{1,0:T(8,128)(2,1)} %all-gather.2.cloned.1.call-done), kind=kOutput, calls=%fused_computation.2 | convolution fusion | flops 377651200 | bytes 2244608 | tf_op jit(solution)/shard_map/dot_general | solution.py:27
  56.5 3.3 %collective-permute-start = (bf16[320,256]{1,0:T(8,128)(2,1)S(1)}, bf16[320,256]{1,0:T(8,128)(2,1)S(1)}, u32[]{:S(2)}, u32[]{:S(2)}) collective-permute-start(bf16[320,256]{1,0:T(8,128)(2,1)S(1)} %constant_dynamic-slice_fusion.2), channel_id=1, source_target_pairs={{0,16},{16,0},{1,17},{17,1},{2,18},{18,2},{3,19},{19,3},{4,20},{20... | collective-permute-start | bytes 491528 | tf_op jit(solution)/shard_map/ppermute | solution.py:125
  59.9 3.1 %collective-permute-done = bf16[320,256]{1,0:T(8,128)(2,1)S(1)} collective-permute-done((bf16[320,256]{1,0:T(8,128)(2,1)S(1)}, bf16[320,256]{1,0:T(8,128)(2,1)S(1)}, u32[]{:S(2)}, u32[]{:S(2)}) %collective-permute-start) | collective-permute-done | bytes 163872 | tf_op jit(solution)/shard_map/ppermute | solution.py:125
  63.0 0.1 broadcast_select_fusion
  63.0 0.0 all-to-all-done.after_ref.qkv_ref
  63.1 0.7 shard_map.94
  63.8 4.4 %reduce-scatter.2.cloned.1.call-done = bf16[144,1152]{1,0:T(8,128)(2,1)} async-done(((bf16[1152,1152]{1,0:T(8,128)(2,1)}), bf16[144,1152]{1,0:T(8,128)(2,1)}) %reduce-scatter.2.cloned.1.call-update) | async-done | bytes 331792 | tf_op jit(solution)/shard_map/reduce_scatter | solution.py:210
  68.2 8.7 %all-to-all-start.1 = ((bf16[16,40,256]{2,1,0:T(8,128)(2,1)}), bf16[16,40,256]{2,1,0:T(8,128)(2,1)S(1)}, u32[]{:S(2)}, u32[]{:S(2)}) async-start(bf16[16,40,256]{2,1,0:T(8,128)(2,1)} %shard_map.94), calls=%async_computation.2 | async-start | bytes 655360 | tf_op jit(solution)/shard_map/all_to_all | solution.py:129
  76.9 1.0 constant_dynamic-slice_fusion
  77.9 4.3 %collective-permute-start.3 = (bf16[72,1152]{1,0:T(8,128)(2,1)S(1)}, bf16[72,1152]{1,0:T(8,128)(2,1)S(1)}, u32[]{:S(2)}, u32[]{:S(2)}) collective-permute-start(bf16[72,1152]{1,0:T(8,128)(2,1)S(1)} %get-tuple-element.24), channel_id=1, source_target_pairs={{0,272},{16,256},{256,16},{272,0},{1,273},{17,257},{257,17},{273,1... | collective-permute-start | bytes 497672 | tf_op jit(solution)/shard_map/ppermute | solution.py:165
  82.3 1.9 %collective-permute-start.1 = (bf16[72,1152]{1,0:T(8,128)(2,1)S(1)}, bf16[72,1152]{1,0:T(8,128)(2,1)S(1)}, u32[]{:S(2)}, u32[]{:S(2)}) collective-permute-start(bf16[72,1152]{1,0:T(8,128)(2,1)S(1)} %get-tuple-element.24), channel_id=1, source_target_pairs={{0,16},{16,0},{256,272},{272,256},{1,17},{17,1},{257,273},{273,257... | collective-permute-start | bytes 497672 | tf_op jit(solution)/shard_map/ppermute | solution.py:165
  84.2 3.4 %collective-permute-start.2 = (bf16[72,1152]{1,0:T(8,128)(2,1)S(1)}, bf16[72,1152]{1,0:T(8,128)(2,1)S(1)}, u32[]{:S(2)}, u32[]{:S(2)}) collective-permute-start(bf16[72,1152]{1,0:T(8,128)(2,1)S(1)} %get-tuple-element.25.a_ref), channel_id=1, source_target_pairs={{0,256},{16,272},{256,0},{272,16},{1,257},{17,273},{257,1},{273,17... | collective-permute-start | bytes 497672 | tf_op jit(solution)/shard_map/ppermute | solution.py:165
  87.6 0.0 collective-permute-done.3.d_ref
  87.6 2.1 %collective-permute-done.1.b_ref = bf16[72,1152]{1,0:T(8,128)(2,1)S(1)} collective-permute-done((bf16[72,1152]{1,0:T(8,128)(2,1)S(1)}, bf16[72,1152]{1,0:T(8,128)(2,1)S(1)}, u32[]{:S(2)}, u32[]{:S(2)}) %collective-permute-start.1) | collective-permute-done | bytes 165920 | tf_op jit(solution)/shard_map/ppermute | solution.py:165
  89.6 3.4 %collective-permute-done.2.c_ref = bf16[72,1152]{1,0:T(8,128)(2,1)S(1)} collective-permute-done((bf16[72,1152]{1,0:T(8,128)(2,1)S(1)}, bf16[72,1152]{1,0:T(8,128)(2,1)S(1)}, u32[]{:S(2)}, u32[]{:S(2)}) %collective-permute-start.2) | collective-permute-done | bytes 165920 | tf_op jit(solution)/shard_map/ppermute | solution.py:165
  93.1 0.0 all-to-all-done.1.g_ref.after_ref
  93.1 0.1 shard_map.96
  93.2 0.7 pad.4
  93.8 8.2 %all-to-all-start.2 = ((bf16[16,48,128]{2,1,0:T(8,128)(2,1)}), bf16[16,48,128]{2,1,0:T(8,128)(2,1)S(1)}, u32[]{:S(2)}, u32[]{:S(2)}) async-start(bf16[16,48,128]{2,1,0:T(8,128)(2,1)} %bitcast.14), calls=%async_computation.3 | async-start | bytes 393216 | tf_op jit(solution)/shard_map/all_to_all | solution.py:129
  102.0 8.0 %shard_map.95 = bf16[16,3,72,128]{3,2,1,0:T(8,128)(2,1)S(1)} custom-call(bf16[16,3,72,128]{3,2,1,0:T(8,128)(2,1)S(1)} %all-to-all-done.after_ref.qkv_ref, bf16[16,40,256]{2,1,0:T(8,128)(2,1)S(1)} %all-to-all-done.1.g_ref.after_ref), custom_call_target="tpu_custom_call" | custom-call | flops 5368709120 | bytes 3145728 | tf_op jit(solution)/shard_map/pallas_call | solution.py:111
  110.1 2.3 %all-to-all-done.2 = bf16[16,48,128]{2,1,0:T(8,128)(2,1)S(1)} async-done(((bf16[16,48,128]{2,1,0:T(8,128)(2,1)}), bf16[16,48,128]{2,1,0:T(8,128)(2,1)S(1)}, u32[]{:S(2)}, u32[]{:S(2)}) %all-to-all-start.2) | async-done | bytes 196640 | tf_op jit(solution)/shard_map/all_to_all | solution.py:129
  112.4 0.1 pad_maximum_fusion
  112.5 34.4 %all_to_all.20 = bf16[16,264,128]{2,1,0:T(8,128)(2,1)S(1)} all-to-all(bf16[16,264,128]{2,1,0:T(8,128)(2,1)S(1)} %pad_maximum_fusion), channel_id=1, replica_groups=mesh['dp'=2,'z'=8,'xl'=2,'y'=8,'core'=2] {'y','core'}, dimensions={0} | all-to-all | bytes 2162688 | tf_op jit(solution)/shard_map/all_to_all | solution.py:129
  146.9 0.1 slice.13
  147.0 1.1 shard_map.97
  148.1 0.7 convert_bitcast_fusion
  (6 shorter events, 0.1 us)
Async XLA Ops:
  8.0 1.0 copy-start
  8.0 46.6 %all-gather.2.cloned.1.call-start = ((), (), s32[]{:S(2)}) async-start(), calls=%async_computation.5 | async-start | bytes 1474560 | tf_op jit(solution)/shard_map/all_gather | solution.py:152
  8.7 59.5 %reduce-scatter.2.cloned.1.call-start = ((), (), s32[]{:S(2)}) async-start(), calls=%async_computation.6 | async-start | bytes 2985984 | tf_op jit(solution)/shard_map/reduce_scatter | solution.py:210
  12.3 1.0 copy-start.1
  12.3 1.0 copy-start.2
  12.3 1.1 copy-start.3
  12.3 2.3 %copy-start.4 = (bf16[72,1152]{1,0:T(8,128)(2,1)S(1)}, bf16[72,1152]{1,0:T(8,128)(2,1)}, u32[]{:S(2)}) copy-start(bf16[72,1152]{1,0:T(8,128)(2,1)} %param.11) | copy-start | bytes 497668
  14.7 48.4 %all-to-all-start = ((bf16[16,3,72,128]{3,2,1,0:T(8,128)(2,1)}), bf16[16,3,72,128]{3,2,1,0:T(8,128)(2,1)S(1)}, u32[]{:S(2)}, u32[]{:S(2)}) async-start(bf16[16,3,72,128]{3,2,1,0:T(8,128)(2,1)} %shard_map.93), calls=%async_computation | async-start | bytes 1769472 | tf_op jit(solution)/shard_map/all_to_all | solution.py:129
  56.5 6.5 %collective-permute-start = (bf16[320,256]{1,0:T(8,128)(2,1)S(1)}, bf16[320,256]{1,0:T(8,128)(2,1)S(1)}, u32[]{:S(2)}, u32[]{:S(2)}) collective-permute-start(bf16[320,256]{1,0:T(8,128)(2,1)S(1)} %constant_dynamic-slice_fusion.2), channel_id=1, source_target_pairs={{0,16},{16,0},{1,17},{17,1},{2,18},{18,2},{3,19},{19,3},{4,20},{20... | collective-permute-start | bytes 491528 | tf_op jit(solution)/shard_map/ppermute | solution.py:125
  68.2 24.8 %all-to-all-start.1 = ((bf16[16,40,256]{2,1,0:T(8,128)(2,1)}), bf16[16,40,256]{2,1,0:T(8,128)(2,1)S(1)}, u32[]{:S(2)}, u32[]{:S(2)}) async-start(bf16[16,40,256]{2,1,0:T(8,128)(2,1)} %shard_map.94), calls=%async_computation.2 | async-start | bytes 655360 | tf_op jit(solution)/shard_map/all_to_all | solution.py:129
  77.9 9.6 %collective-permute-start.3 = (bf16[72,1152]{1,0:T(8,128)(2,1)S(1)}, bf16[72,1152]{1,0:T(8,128)(2,1)S(1)}, u32[]{:S(2)}, u32[]{:S(2)}) collective-permute-start(bf16[72,1152]{1,0:T(8,128)(2,1)S(1)} %get-tuple-element.24), channel_id=1, source_target_pairs={{0,272},{16,256},{256,16},{272,0},{1,273},{17,257},{257,17},{273,1... | collective-permute-start | bytes 497672 | tf_op jit(solution)/shard_map/ppermute | solution.py:165
  82.3 7.4 %collective-permute-start.1 = (bf16[72,1152]{1,0:T(8,128)(2,1)S(1)}, bf16[72,1152]{1,0:T(8,128)(2,1)S(1)}, u32[]{:S(2)}, u32[]{:S(2)}) collective-permute-start(bf16[72,1152]{1,0:T(8,128)(2,1)S(1)} %get-tuple-element.24), channel_id=1, source_target_pairs={{0,16},{16,0},{256,272},{272,256},{1,17},{17,1},{257,273},{273,257... | collective-permute-start | bytes 497672 | tf_op jit(solution)/shard_map/ppermute | solution.py:165
  84.2 8.8 %collective-permute-start.2 = (bf16[72,1152]{1,0:T(8,128)(2,1)S(1)}, bf16[72,1152]{1,0:T(8,128)(2,1)S(1)}, u32[]{:S(2)}, u32[]{:S(2)}) collective-permute-start(bf16[72,1152]{1,0:T(8,128)(2,1)S(1)} %get-tuple-element.25.a_ref), channel_id=1, source_target_pairs={{0,256},{16,272},{256,0},{272,16},{1,257},{17,273},{257,1},{273,17... | collective-permute-start | bytes 497672 | tf_op jit(solution)/shard_map/ppermute | solution.py:165
  93.8 18.5 %all-to-all-start.2 = ((bf16[16,48,128]{2,1,0:T(8,128)(2,1)}), bf16[16,48,128]{2,1,0:T(8,128)(2,1)S(1)}, u32[]{:S(2)}, u32[]{:S(2)}) async-start(bf16[16,48,128]{2,1,0:T(8,128)(2,1)} %bitcast.14), calls=%async_computation.3 | async-start | bytes 393216 | tf_op jit(solution)/shard_map/all_to_all | solution.py:129
Sparse Core Ops, SparseCore 0:
  10.9 33.1 all-gather.1
Sparse Core Ops, SparseCore 1:
  12.4 55.8 reduce-scatter.1

commit v2 on v1

--- a/solution.py
+++ b/solution.py
@@ -1,3 +1,4 @@
+import functools
 import math
 
 import jax
@@ -14,7 +15,8 @@
 TOKENS = 128
 FRAME = 1024
 HALF = 40
-PIECE = 48
+PIECE = 24
+RING = 8
 QUERIES = 256
 SCALE = 1.0 / math.sqrt(HD)
 LOG2E = math.log2(math.e)
@@ -129,75 +131,98 @@
     return lax.all_to_all(x, axis, split_axis=0, concat_axis=0, tiled=True)
 
 
-def interleave_kernel(after_ref, even_ref, odd_ref, out_ref):
-    for i in range(HEADS // 2):
-        out_ref[2 * i] = even_ref[i]
-        out_ref[2 * i + 1] = odd_ref[i]
-
-
-def interleave_after(after, even, odd):
+def along_z(x, apart):
+    return lax.ppermute(x, "z", [(i, i ^ apart) for i in range(RING)])
+
+
+def gather_weights(w_out):
+    core = lax.axis_index("core")
+    blocks = lax.dynamic_slice_in_dim(w_out, (HD - HALF) * core, HALF, axis=0)
+    order = (0,)
+    for apart in (4, 2, 1):
+        blocks = jnp.concatenate([blocks, along_z(blocks, apart)], axis=0)
+        order = order + tuple(r ^ apart for r in order)
+    return blocks, order
+
+
+def interleave_kernel(order, place_ref, after_ref, own_ref, other_ref, out_ref):
+    z, parity = place_ref[0], place_ref[1]
+    for i, r in enumerate(order):
+        first = 2 * lax.bitwise_xor(z, r)
+        out_ref[first + parity] = own_ref[i]
+        out_ref[first + 1 - parity] = other_ref[i]
+
+
+def interleave_after(after, own, other, order):
     vmem = pl.BlockSpec(memory_space=pltpu.VMEM)
-    return pl.pallas_call(
-        interleave_kernel,
+    place = jnp.stack([lax.axis_index("z"), lax.axis_index("xl")])
+    return pl.pallas_call(
+        functools.partial(interleave_kernel, order),
         out_shape=jax.ShapeDtypeStruct((HEADS, HALF, 2 * TOKENS), BF16),
+        in_specs=[
+            pl.BlockSpec(memory_space=pltpu.SMEM),
+            pl.BlockSpec(memory_space=pl.ANY),
+            vmem,
+            vmem,
+        ],
+        compiler_params=pltpu.CompilerParams(vmem_limit_bytes=8 * 2**20),
+        cost_estimate=pl.CostEstimate(flops=0, bytes_accessed=2**20, transcendentals=0),
+    )(place, after, own, other)
+
+
+def head_cotangents(grad_out, beside, weights, order, after):
+    other = dot(weights, beside, 1, 1).astype(BF16)
+    arrived = exchange(other, "xl").reshape(RING, HALF, 2 * TOKENS)
+    own = dot(weights, grad_out, 1, 1).astype(BF16).reshape(RING, HALF, 2 * TOKENS)
+    return interleave_after(after, own, arrived, order)
+
+
+def add(a, b):
+    return (a.astype(F32) + b.astype(F32)).astype(BF16)
+
+
+def sum_terms(attn_out, grad_out, after):
+    parity, z, core = (lax.axis_index(axis) for axis in ("xl", "z", "core"))
+    terms = dot(attn_out, grad_out, 0, 0).astype(BF16).reshape(RING, 2, HD, D)
+
+    def part(which):
+        at = (0, which, (HD - HALF) * core, 0)
+        return lax.dynamic_slice(terms, at, (RING, 1, HALF, D)).reshape(RING, HALF, D)
+
+    total = add(part(parity), exchange(part(1 - parity), "xl"))
+    for apart in (1, 2, 4):
+        mine = (z // apart) % 2
+        halves = total.reshape(4 // apart, 2, HALF, D)
+        arrived = along_z(lax.dynamic_index_in_dim(halves, 1 - mine, 1, keepdims=False), apart)
+        kept = lax.dynamic_index_in_dim(halves, mine, 1, keepdims=False)
+        total = add(kept, arrived) if apart < 4 else add_after(after, kept[0], arrived[0])
+    return total
+
+
+def add_kernel(after_ref, a_ref, b_ref, out_ref):
+    out_ref[...] = (a_ref[...].astype(F32) + b_ref[...].astype(F32)).astype(BF16)
+
+
+def add_after(after, a, b):
+    vmem = pl.BlockSpec(memory_space=pltpu.VMEM)
+    return pl.pallas_call(
+        add_kernel,
+        out_shape=jax.ShapeDtypeStruct(a.shape, BF16),
         in_specs=[pl.BlockSpec(memory_space=pl.ANY), vmem, vmem],
         compiler_params=pltpu.CompilerParams(vmem_limit_bytes=8 * 2**20),
         cost_estimate=pl.CostEstimate(flops=0, bytes_accessed=2**20, transcendentals=0),
-    )(after, even, odd)
-
-
-def head_cotangents(grad_out, w_rows, after):
-    parity = lax.axis_index("xl")
-    gathered = lax.all_gather(w_rows, "z", axis=0, tiled=True)
-    tokens = lax.all_gather(grad_out, ("xl", "core"), axis=0, tiled=True)
-    both = dot(gathered, tokens, 1, 1).astype(BF16)
-    own = lax.dynamic_slice_in_dim(both, 2 * TOKENS * parity, 2 * TOKENS, axis=1)
-    other = lax.dynamic_slice_in_dim(both, 2 * TOKENS * (1 - parity), 2 * TOKENS, axis=1)
-    arrived = exchange(other, "xl").reshape(HEADS // 2, HALF, 2 * TOKENS)
-    own = own.reshape(HEADS // 2, HALF, 2 * TOKENS)
-    even = jnp.where(parity == 0, own, arrived)
-    odd = jnp.where(parity == 0, arrived, own)
-    return interleave_after(after, even, odd)
-
-
-def along_x(x, flip_dp, flip_xl):
-    pairs = [(2 * a + b, 2 * (a ^ flip_dp) + (b ^ flip_xl)) for a in (0, 1) for b in (0, 1)]
-    return lax.ppermute(x, ("dp", "xl"), pairs)
-
-
-def add_kernel(after_ref, a_ref, b_ref, c_ref, d_ref, out_ref):
-    total = a_ref[...].astype(F32) + b_ref[...].astype(F32)
-    total = total + c_ref[...].astype(F32) + d_ref[...].astype(F32)
-    out_ref[...] = total.astype(BF16)
-
-
-def add_after(after, parts):
-    vmem = pl.BlockSpec(memory_space=pltpu.VMEM)
-    return pl.pallas_call(
-        add_kernel,
-        out_shape=jax.ShapeDtypeStruct(parts[0].shape, BF16),
-        in_specs=[pl.BlockSpec(memory_space=pl.ANY)] + [vmem] * 4,
-        compiler_params=pltpu.CompilerParams(vmem_limit_bytes=8 * 2**20),
-        cost_estimate=pl.CostEstimate(flops=0, bytes_accessed=2**20, transcendentals=0),
-    )(after, *parts)
-
-
-def sum_along_x(rows, after):
-    parity = lax.axis_index("xl")
-    own = lax.dynamic_slice_in_dim(rows, HD * parity, HD, axis=0)
-    other = lax.dynamic_slice_in_dim(rows, HD * (1 - parity), HD, axis=0)
-    parts = (own, along_x(other, 0, 1), along_x(own, 1, 0), along_x(other, 1, 1))
-    return add_after(after, parts)
+    )(after, a, b)
 
 
 def to_pieces(x):
-    tiles = x.reshape(9, 8, 9, 128).transpose(0, 2, 1, 3).reshape(81, 8, 128)
-    return jnp.pad(tiles, ((0, 15), (0, 0), (0, 0))).reshape(HEADS, PIECE, 128)
+    tiles = x.reshape(5, 8, 9, 128).transpose(0, 2, 1, 3).reshape(45, 8, 128)
+    return jnp.pad(tiles, ((0, 3), (0, 0), (0, 0))).reshape(HEADS, PIECE, 128)
 
 
 def from_pieces(x):
-    tiles = x.reshape(96, 8, 128)[:81].reshape(9, 9, 8, 128)
-    return tiles.transpose(0, 2, 1, 3).reshape(HD, D)
+    tiles = x.transpose(1, 0, 2, 3).reshape(2, 48, 8, 128)[:, :45]
+    halves = tiles.reshape(2, 5, 9, 8, 128).transpose(0, 1, 3, 2, 4).reshape(2, HALF, D)
+    return jnp.concatenate([halves[0], halves[1, 2 * HALF - HD :]], axis=0)
 
 
 def shards(queries, key_states, value_states, grad_out, attn_out, w_out):
@@ -205,27 +230,27 @@
     q, k, v, grad_out, attn_out = (
         a.reshape(TOKENS, D) for a in (queries, key_states, value_states, grad_out, attn_out)
     )
-    core = lax.axis_index("core")
-    term = dot(attn_out, grad_out, 0, 0).astype(BF16)
-    rows = lax.psum_scatter(term, "z", scatter_dimension=0, tiled=True)
-    w_rows = lax.dynamic_slice_in_dim(w_out, (HD - HALF) * core, HALF, axis=0)
-    packed, w_rows = lax.optimization_barrier((pack(q, k, v), w_rows))
-    qkv = all_to_all(packed, SPACE)
-    g = head_cotangents(grad_out, w_rows, qkv)
-    g, rows = lax.optimization_barrier((g, rows))
-    g = all_to_all(g, SPACE)
-    pieces = all_to_all(to_pieces(sum_along_x(rows, g)), SPACE)
-    piece = jnp.sum(pieces.astype(F32), axis=0, keepdims=True).astype(BF16)
+    weights, order = gather_weights(w_out)
+    beside = exchange(grad_out, "xl")
+    qkv = all_to_all(pack(q, k, v), SPACE)
+    grad_out, beside, attn_out = (
+        lax.all_gather(a, "core", axis=0, tiled=True) for a in (grad_out, beside, attn_out)
+    )
+    g = all_to_all(head_cotangents(grad_out, beside, weights, order, qkv), SPACE)
+    rows = to_pieces(sum_terms(attn_out, grad_out, g))
+    pieces = all_to_all(jnp.concatenate([rows, rows]), ("dp", "y", "core"))
+    piece = jnp.sum(pieces.reshape(HEADS, 2, PIECE, 128).astype(F32), axis=0).astype(BF16)
+    piece = piece.reshape(1, 2 * PIECE, 128)
     sent = jnp.concatenate(
         [
             attention(qkv, g).reshape(HEADS, 3 * HD, 128),
-            jnp.broadcast_to(piece, (HEADS, PIECE, 128)),
+            jnp.broadcast_to(piece, (HEADS, 2 * PIECE, 128)),
         ],
         axis=1,
     )
     arrived = all_to_all(sent, SPACE)
     grads = unpack(arrived[:, : 3 * HD].reshape(HEADS, 3, HD, TOKENS))
-    grad_w_out = from_pieces(arrived[:, 3 * HD :].astype(F32))
+    grad_w_out = from_pieces(arrived[:, 3 * HD :].astype(F32).reshape(HEADS, 2, PIECE, 128))
     return tuple(a.reshape(local_shape) for a in grads) + (grad_w_out,)
 
 

time: 157 us -> 144 us (0.917)
  blocking collectives: 64 us -> 42.7 us
  starting transfers between devices: 40.2 us -> 57.3 us
  between operations: 15.6 us -> 0.99 us
  waiting for transfers between devices: 16 us -> 22.8 us
  matrix products: 5.24 us -> 1.8 us
  other arithmetic: 0.95 us -> 3.39 us
    all_gather x1 -> x3, blocking collectives: 29.6 us -> 8.72 us  [shards(): lax.all_gather(a, 'core', axis=0, tiled=True)]
    ppermute x3 -> x6, starting transfers between devices: 9.61 us -> 24.9 us  [along_z(): return lax.ppermute(x, 'z', [(i, i ^ apart) for i in range(RING)])]
    ppermute x3 -> x6, waiting for transfers between devices: 5.46 us -> 14.5 us  [along_z(): return lax.ppermute(x, 'z', [(i, i ^ apart) for i in range(RING)])]
    all_to_all x3, waiting for transfers between devices: 2.28 us -> 8.26 us  [all_to_all(): return lax.all_to_all(x, axis, split_axis=0, concat_axis=0, tiled=True)]
    ppermute x1 -> x3, starting transfers between devices: 3.34 us -> 8.41 us  [exchange(): return lax.ppermute(x, axis, [(0, 1), (1, 0)])]
    reduce_scatter x1 -> x0, waiting for transfers between devices: 4.43 us -> none  [shards(): rows = lax.psum_scatter(term, 'z', scatter_dimension=0, tiled=True)]
    dot_general x2 -> x3, matrix products: 5.24 us -> 1.8 us  [dot(): lax.dot_general(a, b, (((dim_a,), (dim_b,)), ((), ())), preferred_element...]
    all_to_all x3, starting transfers between devices: 27.2 us -> 24.1 us  [all_to_all(): return lax.all_to_all(x, axis, split_axis=0, concat_axis=0, tiled=True)]
  transfers between devices with their start and end apart: 9 -> 12, of which waited for: 5 -> 8; matrix products, arithmetic and copies ran while one was open for 4% -> 3% of each run, Pallas kernels for 6% -> 7%
where the time goes in v2:
time: 144 us; the launch traced here: 143 us
  starting transfers between devices  57.3 us (40%)
  blocking collectives  42.7 us (30%)
  waiting for transfers between devices  22.8 us (16%)
  Pallas kernels  11.7 us (8%)
  other arithmetic  3.39 us (2%)
  local copies, waits for them, and re-layouts  2.71 us (2%)
  matrix products  1.8 us (1%)
    all_to_all x1, blocking collectives, all_to_all(): return lax.all_to_all(x, axis, split_axis=0, concat_axis=0, tiled=True)  34 us
    ppermute x6, starting transfers between devices, along_z(): return lax.ppermute(x, 'z', [(i, i ^ apart) for i in range(RING)])  24.9 us
    all_to_all x3, starting transfers between devices, all_to_all(): return lax.all_to_all(x, axis, split_axis=0, concat_axis=0, tiled=True)  24.1 us
    ppermute x6, waiting for transfers between devices, along_z(): return lax.ppermute(x, 'z', [(i, i ^ apart) for i in range(RING)])  14.5 us
    all_gather x3, blocking collectives, shards(): lax.all_gather(a, 'core', axis=0, tiled=True)  8.72 us
    ppermute x3, starting transfers between devices, exchange(): return lax.ppermute(x, axis, [(0, 1), (1, 0)])  8.41 us
    all_to_all x3, waiting for transfers between devices, all_to_all(): return lax.all_to_all(x, axis, split_axis=0, concat_axis=0, tiled=True)  8.26 us
    pallas_call x1, Pallas kernels, attention(): pl.pallas_call(attention_kernel, out_shape=jax.ShapeDtypeStruct((HEADS, 3...  8.06 us
  transfers between devices with their start and end apart: 12, of which 8 were waited for; matrix products, arithmetic and copies ran while one was open for 3% of the time, Pallas kernels for 7%

profile of v2, /device:TPU:1, one launch (start us, length us, event | category | flops | bytes accessed | tf_op | source)
XLA Modules:
  0.0 143.4 jit_solution(2341826655861785992)
XLA Ops:
  0.6 0.0 copy-start
  0.7 0.9 copy-done
  1.6 11.5 %collective-permute-start = (bf16[40,1152]{1,0:T(8,128)(2,1)S(1)}, bf16[40,1152]{1,0:T(8,128)(2,1)S(1)}, u32[]{:S(2)}, u32[]{:S(2)}) collective-permute-start(bf16[40,1152]{1,0:T(8,128)(2,1)S(1)} %constant_dynamic-slice_fusion.1), channel_id=1, source_target_pairs={{0,128},{32,160},{64,192},{96,224},{128,0},{160,32},{192,64},{224,... | collective-permute-start | bytes 276488 | tf_op jit(solution)/shard_map/ppermute | solution.py:135
  13.0 3.0 %all_gather.9 = bf16[256,1152]{1,0:T(8,128)(2,1)S(1)} all-gather(bf16[128,1152]{1,0:T(8,128)(2,1)} %bitcast.93), channel_id=1, replica_groups=mesh['dp'=2,'z'=8,'xl'=2,'y'=8,'core'=2] {'core'}, dimensions={0}, use_global_device_ids=true | all-gather | bytes 884736 | tf_op jit(solution)/shard_map/all_gather | solution.py:237
  16.1 2.4 %all_gather.11 = bf16[256,1152]{1,0:T(8,128)(2,1)S(1)} all-gather(bf16[128,1152]{1,0:T(8,128)(2,1)} %bitcast.92), channel_id=1, replica_groups=mesh['dp'=2,'z'=8,'xl'=2,'y'=8,'core'=2] {'core'}, dimensions={0}, use_global_device_ids=true | all-gather | bytes 884736 | tf_op jit(solution)/shard_map/all_gather | solution.py:237
  18.5 1.0 convolution_convert_fusion
  19.5 0.0 copy-start.5
  19.5 0.0 copy-start.1
  19.5 0.0 copy-start.2
  19.5 0.0 copy-start.3
  19.5 1.4 %copy-done.4 = bf16[1152,1152]{1,0:T(8,128)(2,1)} copy-done((bf16[1152,1152]{1,0:T(8,128)(2,1)}, bf16[1152,1152]{1,0:T(8,128)(2,1)S(1)}, u32[]{:S(2)}) %copy-start.4) | copy-done | bytes 2654232
  21.0 0.1 dynamic-slice_bitcast_fusion
  21.0 3.1 %collective-permute-start.5 = (bf16[8,40,1152]{2,1,0:T(8,128)(2,1)S(1)}, bf16[8,40,1152]{2,1,0:T(8,128)(2,1)}, u32[]{:S(2)}, u32[]{:S(2)}) collective-permute-start(bf16[8,40,1152]{2,1,0:T(8,128)(2,1)S(1)} %dynamic-slice_bitcast_fusion), channel_id=1, source_target_pairs={{0,16},{16,0},{1,17},{17,1},{2,18},{18,2},{3,19},{19,3},{4,20},{20... | collective-permute-start | bytes 2211848 | tf_op jit(solution)/shard_map/ppermute | solution.py:127
  24.2 0.0 collective-permute-done
  24.2 4.0 %collective-permute-start.1 = (bf16[80,1152]{1,0:T(8,128)(2,1)S(1)}, bf16[80,1152]{1,0:T(8,128)(2,1)S(1)}, u32[]{:S(2)}, u32[]{:S(2)}) collective-permute-start(bf16[80,1152]{1,0:T(8,128)(2,1)S(1)} %pad_maximum_fusion.5), channel_id=1, source_target_pairs={{0,64},{32,96},{64,0},{96,32},{128,192},{160,224},{192,128},{224,1... | collective-permute-start | bytes 552968 | tf_op jit(solution)/shard_map/ppermute | solution.py:135
  28.2 2.2 %collective-permute-start.3 = (bf16[128,1152]{1,0:T(8,128)(2,1)S(1)}, bf16[128,1152]{1,0:T(8,128)(2,1)}, u32[]{:S(2)}, u32[]{:S(2)}) collective-permute-start(bf16[128,1152]{1,0:T(8,128)(2,1)S(1)} %bitcast.94), channel_id=1, source_target_pairs={{0,16},{16,0},{1,17},{17,1},{2,18},{18,2},{3,19},{19,3},{4,20},{20... | collective-permute-start | bytes 884744 | tf_op jit(solution)/shard_map/ppermute | solution.py:127
  30.4 1.2 shard_map.93
  31.7 8.3 %all-to-all-start = ((bf16[16,3,72,128]{3,2,1,0:T(8,128)(2,1)}), bf16[16,3,72,128]{3,2,1,0:T(8,128)(2,1)S(1)}, u32[]{:S(2)}, u32[]{:S(2)}) async-start(bf16[16,3,72,128]{3,2,1,0:T(8,128)(2,1)} %shard_map.93), calls=%async_computation | async-start | bytes 1769472 | tf_op jit(solution)/shard_map/all_to_all | solution.py:131
  40.0 0.1 pad_add_fusion.place_ref
  40.1 3.1 %collective-permute-start.2 = (bf16[160,1152]{1,0:T(8,128)(2,1)S(1)}, bf16[160,1152]{1,0:T(8,128)(2,1)S(1)}, u32[]{:S(2)}, u32[]{:S(2)}) collective-permute-start(bf16[160,1152]{1,0:T(8,128)(2,1)S(1)} %pad_maximum_fusion.2), channel_id=1, source_target_pairs={{0,32},{32,0},{64,96},{96,64},{128,160},{160,128},{192,224},{224,1... | collective-permute-start | bytes 1105928 | tf_op jit(solution)/shard_map/ppermute | solution.py:135
  43.2 1.5 %fusion = bf16[8,40,1152]{2,1,0:T(8,128)(2,1)S(1)} fusion(bf16[8,40,1152]{2,1,0:T(8,128)(2,1)} %collective-permute-done.5, bf16[8,2,72,1152]{3,2,1,0:T(8,128)(2,1)} %bitcast.82, s32[]{:T(128)S(6)} %select_n.56, s32[]{:T(128)S(6)} %select_n.55), kind=kLoop, calls=%fused_computation.2 | loop fusion | flops 1474560 | bytes 2211848 | tf_op jit(solution)/shard_map/convert_element_type | solution.py:181
  44.8 2.2 %collective-permute-start.6 = (bf16[4,40,1152]{2,1,0:T(8,128)(2,1)S(1)}, bf16[4,40,1152]{2,1,0:T(8,128)(2,1)S(1)}, u32[]{:S(2)}, u32[]{:S(2)}) collective-permute-start(bf16[4,40,1152]{2,1,0:T(8,128)(2,1)S(1)} %dynamic-slice_bitcast_fusion.1), channel_id=1, source_target_pairs={{0,32},{32,0},{64,96},{96,64},{128,160},{160,128},{192,224},{224,1... | collective-permute-start | bytes 1105928 | tf_op jit(solution)/shard_map/ppermute | solution.py:135
  47.0 0.1 collective-permute-done.3
  47.1 3.3 %all_gather.10 = bf16[256,1152]{1,0:T(8,128)(2,1)S(1)} all-gather(bf16[128,1152]{1,0:T(8,128)(2,1)} %collective-permute-done.3), channel_id=1, replica_groups=mesh['dp'=2,'z'=8,'xl'=2,'y'=8,'core'=2] {'core'}, dimensions={0}, use_global_device_ids=true | all-gather | bytes 884736 | tf_op jit(solution)/shard_map/all_gather | solution.py:237
  50.3 1.7 %collective-permute-done.2 = bf16[160,1152]{1,0:T(8,128)(2,1)S(1)} collective-permute-done((bf16[160,1152]{1,0:T(8,128)(2,1)S(1)}, bf16[160,1152]{1,0:T(8,128)(2,1)S(1)}, u32[]{:S(2)}, u32[]{:S(2)}) %collective-permute-start.2) | collective-permute-done | bytes 368672 | tf_op jit(solution)/shard_map/ppermute | solution.py:135
  52.0 0.4 convolution_convert_fusion.1
  52.4 3.1 %collective-permute-start.4 = (bf16[320,256]{1,0:T(8,128)(2,1)S(1)}, bf16[320,256]{1,0:T(8,128)(2,1)S(1)}, u32[]{:S(2)}, u32[]{:S(2)}) collective-permute-start(bf16[320,256]{1,0:T(8,128)(2,1)S(1)} %convolution_convert_fusion.1), channel_id=1, source_target_pairs={{0,16},{16,0},{1,17},{17,1},{2,18},{18,2},{3,19},{19,3},{4,20},{20... | collective-permute-start | bytes 491528 | tf_op jit(solution)/shard_map/ppermute | solution.py:127
  55.6 4.3 %collective-permute-done.6 = bf16[4,40,1152]{2,1,0:T(8,128)(2,1)S(1)} collective-permute-done((bf16[4,40,1152]{2,1,0:T(8,128)(2,1)S(1)}, bf16[4,40,1152]{2,1,0:T(8,128)(2,1)S(1)}, u32[]{:S(2)}, u32[]{:S(2)}) %collective-permute-start.6) | collective-permute-done | bytes 368672 | tf_op jit(solution)/shard_map/ppermute | solution.py:135
  59.9 0.1 fusion.1
  60.1 2.2 %collective-permute-start.7 = (bf16[2,40,1152]{2,1,0:T(8,128)(2,1)S(1)}, bf16[2,40,1152]{2,1,0:T(8,128)(2,1)S(1)}, u32[]{:S(2)}, u32[]{:S(2)}) collective-permute-start(bf16[2,40,1152]{2,1,0:T(8,128)(2,1)S(1)} %dynamic-slice_bitcast_fusion.2), channel_id=1, source_target_pairs={{0,64},{32,96},{64,0},{96,32},{128,192},{160,224},{192,128},{224,1... | collective-permute-start | bytes 552968 | tf_op jit(solution)/shard_map/ppermute | solution.py:135
  62.2 0.4 convolution_convert_fusion.2
  62.7 2.0 %all-to-all-done.after_ref.qkv_ref = bf16[16,3,72,128]{3,2,1,0:T(8,128)(2,1)S(1)} async-done(((bf16[16,3,72,128]{3,2,1,0:T(8,128)(2,1)}), bf16[16,3,72,128]{3,2,1,0:T(8,128)(2,1)S(1)}, u32[]{:S(2)}, u32[]{:S(2)}) %all-to-all-start) | async-done | bytes 884768 | tf_op jit(solution)/shard_map/all_to_all | solution.py:131
  64.6 1.3 shard_map.94
  65.9 6.2 %all-to-all-start.1 = ((bf16[16,40,256]{2,1,0:T(8,128)(2,1)}), bf16[16,40,256]{2,1,0:T(8,128)(2,1)S(1)}, u32[]{:S(2)}, u32[]{:S(2)}) async-start(bf16[16,40,256]{2,1,0:T(8,128)(2,1)} %shard_map.94), calls=%async_computation.1 | async-start | bytes 655360 | tf_op jit(solution)/shard_map/all_to_all | solution.py:131
  72.1 0.3 collective-permute-done.7
  72.5 1.9 %collective-permute-start.8 = (bf16[1,40,1152]{2,1,0:T(8,128)(2,1)S(1)}, bf16[1,40,1152]{2,1,0:T(8,128)(2,1)S(1)}, u32[]{:S(2)}, u32[]{:S(2)}) collective-permute-start(bf16[1,40,1152]{2,1,0:T(8,128)(2,1)S(1)} %get-tuple-element.24), channel_id=1, source_target_pairs={{0,128},{32,160},{64,192},{96,224},{128,0},{160,32},{192,64},{224,... | collective-permute-start | bytes 276488 | tf_op jit(solution)/shard_map/ppermute | solution.py:135
  74.4 8.2 %collective-permute-done.8 = bf16[1,40,1152]{2,1,0:T(8,128)(2,1)S(1)} collective-permute-done((bf16[1,40,1152]{2,1,0:T(8,128)(2,1)S(1)}, bf16[1,40,1152]{2,1,0:T(8,128)(2,1)S(1)}, u32[]{:S(2)}, u32[]{:S(2)}) %collective-permute-start.8) | collective-permute-done | bytes 92192 | tf_op jit(solution)/shard_map/ppermute | solution.py:135
  82.5 2.6 %all-to-all-done.1.g_ref.after_ref = bf16[16,40,256]{2,1,0:T(8,128)(2,1)S(1)} async-done(((bf16[16,40,256]{2,1,0:T(8,128)(2,1)}), bf16[16,40,256]{2,1,0:T(8,128)(2,1)S(1)}, u32[]{:S(2)}, u32[]{:S(2)}) %all-to-all-start.1) | async-done | bytes 327712 | tf_op jit(solution)/shard_map/all_to_all | solution.py:131
  85.2 0.7 pad_maximum_fusion.4
  85.9 9.6 %all-to-all-start.2 = ((bf16[32,24,128]{2,1,0:T(8,128)(2,1)}), bf16[32,24,128]{2,1,0:T(8,128)(2,1)S(1)}, u32[]{:S(2)}, u32[]{:S(2)}) async-start(bf16[32,24,128]{2,1,0:T(8,128)(2,1)} %pad_maximum_fusion.4), calls=%async_computation.2 | async-start | bytes 393216 | tf_op jit(solution)/shard_map/all_to_all | solution.py:131
  95.5 8.1 %shard_map.95 = bf16[16,3,72,128]{3,2,1,0:T(8,128)(2,1)S(1)} custom-call(bf16[16,3,72,128]{3,2,1,0:T(8,128)(2,1)S(1)} %all-to-all-done.after_ref.qkv_ref, bf16[16,40,256]{2,1,0:T(8,128)(2,1)S(1)} %all-to-all-done.1.g_ref.after_ref), custom_call_target="tpu_custom_call" | custom-call | flops 5368709120 | bytes 3145728 | tf_op jit(solution)/shard_map/pallas_call | solution.py:113
  103.6 3.6 %all-to-all-done.2 = bf16[32,24,128]{2,1,0:T(8,128)(2,1)S(1)} async-done(((bf16[32,24,128]{2,1,0:T(8,128)(2,1)}), bf16[32,24,128]{2,1,0:T(8,128)(2,1)S(1)}, u32[]{:S(2)}, u32[]{:S(2)}) %all-to-all-start.2) | async-done | bytes 196640 | tf_op jit(solution)/shard_map/all_to_all | solution.py:131
  107.3 0.1 pad_maximum_fusion
  107.4 34.0 %all_to_all.20 = bf16[16,264,128]{2,1,0:T(8,128)(2,1)S(1)} all-to-all(bf16[16,264,128]{2,1,0:T(8,128)(2,1)S(1)} %pad_maximum_fusion), channel_id=1, replica_groups=mesh['dp'=2,'z'=8,'xl'=2,'y'=8,'core'=2] {'y','core'}, dimensions={0} | all-to-all | bytes 2162688 | tf_op jit(solution)/shard_map/all_to_all | solution.py:131
  141.4 0.1 convert_bitcast_fusion.1
  141.5 0.1 slice.22
  141.6 1.1 shard_map.97
  142.6 0.7 pad_maximum_fusion.3
  (24 shorter events, 0.4 us)
Async XLA Ops:
  0.6 0.9 copy-start
  1.6 22.6 %collective-permute-start = (bf16[40,1152]{1,0:T(8,128)(2,1)S(1)}, bf16[40,1152]{1,0:T(8,128)(2,1)S(1)}, u32[]{:S(2)}, u32[]{:S(2)}) collective-permute-start(bf16[40,1152]{1,0:T(8,128)(2,1)S(1)} %constant_dynamic-slice_fusion.1), channel_id=1, source_target_pairs={{0,128},{32,160},{64,192},{96,224},{128,0},{160,32},{192,64},{224,... | collective-permute-start | bytes 276488 | tf_op jit(solution)/shard_map/ppermute | solution.py:135
  19.5 1.5 %copy-start.4 = (bf16[1152,1152]{1,0:T(8,128)(2,1)}, bf16[1152,1152]{1,0:T(8,128)(2,1)S(1)}, u32[]{:S(2)}) copy-start(bf16[1152,1152]{1,0:T(8,128)(2,1)S(1)} %convolution_convert_fusion) | copy-start | bytes 7962628
  19.5 8.7 %copy-start.5 = (bf16[2,1,2,32,1152]{4,3,2,1,0:T(8,128)(2,1)S(1)}, bf16[2,1,2,32,1152]{4,3,2,1,0:T(8,128)(2,1)}, u32[]{:S(2)}) copy-start(bf16[2,1,2,32,1152]{4,3,2,1,0:T(8,128)(2,1)} %param.9) | copy-start | bytes 884740
  19.5 10.9 %copy-start.1 = (bf16[2,1,2,32,1152]{4,3,2,1,0:T(8,128)(2,1)S(1)}, bf16[2,1,2,32,1152]{4,3,2,1,0:T(8,128)(2,1)}, u32[]{:S(2)}) copy-start(bf16[2,1,2,32,1152]{4,3,2,1,0:T(8,128)(2,1)} %param.6) | copy-start | bytes 884740
  19.5 10.9 %copy-start.2 = (bf16[2,1,2,32,1152]{4,3,2,1,0:T(8,128)(2,1)S(1)}, bf16[2,1,2,32,1152]{4,3,2,1,0:T(8,128)(2,1)}, u32[]{:S(2)}) copy-start(bf16[2,1,2,32,1152]{4,3,2,1,0:T(8,128)(2,1)} %param.7) | copy-start | bytes 884740
  19.5 10.9 %copy-start.3 = (bf16[2,1,2,32,1152]{4,3,2,1,0:T(8,128)(2,1)S(1)}, bf16[2,1,2,32,1152]{4,3,2,1,0:T(8,128)(2,1)}, u32[]{:S(2)}) copy-start(bf16[2,1,2,32,1152]{4,3,2,1,0:T(8,128)(2,1)} %param.8) | copy-start | bytes 884740
  21.0 22.2 %collective-permute-start.5 = (bf16[8,40,1152]{2,1,0:T(8,128)(2,1)S(1)}, bf16[8,40,1152]{2,1,0:T(8,128)(2,1)}, u32[]{:S(2)}, u32[]{:S(2)}) collective-permute-start(bf16[8,40,1152]{2,1,0:T(8,128)(2,1)S(1)} %dynamic-slice_bitcast_fusion), channel_id=1, source_target_pairs={{0,16},{16,0},{1,17},{17,1},{2,18},{18,2},{3,19},{19,3},{4,20},{20... | collective-permute-start | bytes 2211848 | tf_op jit(solution)/shard_map/ppermute | solution.py:127
  24.2 15.9 %collective-permute-start.1 = (bf16[80,1152]{1,0:T(8,128)(2,1)S(1)}, bf16[80,1152]{1,0:T(8,128)(2,1)S(1)}, u32[]{:S(2)}, u32[]{:S(2)}) collective-permute-start(bf16[80,1152]{1,0:T(8,128)(2,1)S(1)} %pad_maximum_fusion.5), channel_id=1, source_target_pairs={{0,64},{32,96},{64,0},{96,32},{128,192},{160,224},{192,128},{224,1... | collective-permute-start | bytes 552968 | tf_op jit(solution)/shard_map/ppermute | solution.py:135
  28.2 18.8 %collective-permute-start.3 = (bf16[128,1152]{1,0:T(8,128)(2,1)S(1)}, bf16[128,1152]{1,0:T(8,128)(2,1)}, u32[]{:S(2)}, u32[]{:S(2)}) collective-permute-start(bf16[128,1152]{1,0:T(8,128)(2,1)S(1)} %bitcast.94), channel_id=1, source_target_pairs={{0,16},{16,0},{1,17},{17,1},{2,18},{18,2},{3,19},{19,3},{4,20},{20... | collective-permute-start | bytes 884744 | tf_op jit(solution)/shard_map/ppermute | solution.py:127
  31.7 33.0 %all-to-all-start = ((bf16[16,3,72,128]{3,2,1,0:T(8,128)(2,1)}), bf16[16,3,72,128]{3,2,1,0:T(8,128)(2,1)S(1)}, u32[]{:S(2)}, u32[]{:S(2)}) async-start(bf16[16,3,72,128]{3,2,1,0:T(8,128)(2,1)} %shard_map.93), calls=%async_computation | async-start | bytes 1769472 | tf_op jit(solution)/shard_map/all_to_all | solution.py:131
  40.1 11.9 %collective-permute-start.2 = (bf16[160,1152]{1,0:T(8,128)(2,1)S(1)}, bf16[160,1152]{1,0:T(8,128)(2,1)S(1)}, u32[]{:S(2)}, u32[]{:S(2)}) collective-permute-start(bf16[160,1152]{1,0:T(8,128)(2,1)S(1)} %pad_maximum_fusion.2), channel_id=1, source_target_pairs={{0,32},{32,0},{64,96},{96,64},{128,160},{160,128},{192,224},{224,1... | collective-permute-start | bytes 1105928 | tf_op jit(solution)/shard_map/ppermute | solution.py:135
  44.8 15.1 %collective-permute-start.6 = (bf16[4,40,1152]{2,1,0:T(8,128)(2,1)S(1)}, bf16[4,40,1152]{2,1,0:T(8,128)(2,1)S(1)}, u32[]{:S(2)}, u32[]{:S(2)}) collective-permute-start(bf16[4,40,1152]{2,1,0:T(8,128)(2,1)S(1)} %dynamic-slice_bitcast_fusion.1), channel_id=1, source_target_pairs={{0,32},{32,0},{64,96},{96,64},{128,160},{160,128},{192,224},{224,1... | collective-permute-start | bytes 1105928 | tf_op jit(solution)/shard_map/ppermute | solution.py:135
  52.4 10.2 %collective-permute-start.4 = (bf16[320,256]{1,0:T(8,128)(2,1)S(1)}, bf16[320,256]{1,0:T(8,128)(2,1)S(1)}, u32[]{:S(2)}, u32[]{:S(2)}) collective-permute-start(bf16[320,256]{1,0:T(8,128)(2,1)S(1)} %convolution_convert_fusion.1), channel_id=1, source_target_pairs={{0,16},{16,0},{1,17},{17,1},{2,18},{18,2},{3,19},{19,3},{4,20},{20... | collective-permute-start | bytes 491528 | tf_op jit(solution)/shard_map/ppermute | solution.py:127
  60.1 12.3 %collective-permute-start.7 = (bf16[2,40,1152]{2,1,0:T(8,128)(2,1)S(1)}, bf16[2,40,1152]{2,1,0:T(8,128)(2,1)S(1)}, u32[]{:S(2)}, u32[]{:S(2)}) collective-permute-start(bf16[2,40,1152]{2,1,0:T(8,128)(2,1)S(1)} %dynamic-slice_bitcast_fusion.2), channel_id=1, source_target_pairs={{0,64},{32,96},{64,0},{96,32},{128,192},{160,224},{192,128},{224,1... | collective-permute-start | bytes 552968 | tf_op jit(solution)/shard_map/ppermute | solution.py:135
  65.9 19.2 %all-to-all-start.1 = ((bf16[16,40,256]{2,1,0:T(8,128)(2,1)}), bf16[16,40,256]{2,1,0:T(8,128)(2,1)S(1)}, u32[]{:S(2)}, u32[]{:S(2)}) async-start(bf16[16,40,256]{2,1,0:T(8,128)(2,1)} %shard_map.94), calls=%async_computation.1 | async-start | bytes 655360 | tf_op jit(solution)/shard_map/all_to_all | solution.py:131
  72.5 10.1 %collective-permute-start.8 = (bf16[1,40,1152]{2,1,0:T(8,128)(2,1)S(1)}, bf16[1,40,1152]{2,1,0:T(8,128)(2,1)S(1)}, u32[]{:S(2)}, u32[]{:S(2)}) collective-permute-start(bf16[1,40,1152]{2,1,0:T(8,128)(2,1)S(1)} %get-tuple-element.24), channel_id=1, source_target_pairs={{0,128},{32,160},{64,192},{96,224},{128,0},{160,32},{192,64},{224,... | collective-permute-start | bytes 276488 | tf_op jit(solution)/shard_map/ppermute | solution.py:135
  85.9 21.3 %all-to-all-start.2 = ((bf16[32,24,128]{2,1,0:T(8,128)(2,1)}), bf16[32,24,128]{2,1,0:T(8,128)(2,1)S(1)}, u32[]{:S(2)}, u32[]{:S(2)}) async-start(bf16[32,24,128]{2,1,0:T(8,128)(2,1)} %pad_maximum_fusion.4), calls=%async_computation.2 | async-start | bytes 393216 | tf_op jit(solution)/shard_map/all_to_all | solution.py:131

commit v3 on v2

--- a/solution.py
+++ b/solution.py
@@ -181,15 +181,40 @@
     return (a.astype(F32) + b.astype(F32)).astype(BF16)
 
 
+def term_kernel(place_ref, a_ref, g_ref, own_ref, other_ref, turned):
+    turned[...] = a_ref[...].astype(F32).T
+    rows = []
+    for j in range(2):
+        for i in range(RING):
+            first = pl.multiple_of(2 * HD * i + place_ref[j], 8)
+            rows.append(turned[pl.ds(first, HALF), :])
+    result = dot(jnp.concatenate(rows, axis=0).astype(BF16), g_ref[...], 1, 0)
+    for i in range(RING):
+        own_ref[i] = result[HALF * i : HALF * (i + 1)].astype(BF16)
+        other_ref[i] = result[HALF * (RING + i) : HALF * (RING + i + 1)].astype(BF16)
+
+
+def terms(attn_out, grad_out):
+    parity, core = lax.axis_index("xl"), lax.axis_index("core")
+    place = jnp.stack([parity, 1 - parity]) * HD + (HD - HALF) * core
+    vmem = pl.BlockSpec(memory_space=pltpu.VMEM)
+    out = jax.ShapeDtypeStruct((RING, HALF, D), BF16)
+    return pl.pallas_call(
+        term_kernel,
+        out_shape=(out, out),
+        in_specs=[pl.BlockSpec(memory_space=pltpu.SMEM), vmem, vmem],
+        scratch_shapes=[pltpu.VMEM((D, 2 * TOKENS), F32)],
+        compiler_params=pltpu.CompilerParams(vmem_limit_bytes=24 * 2**20),
+        cost_estimate=pl.CostEstimate(
+            flops=4 * RING * HALF * D * 2 * TOKENS, bytes_accessed=3 * 2**20, transcendentals=0
+        ),
+    )(place, attn_out, grad_out)
+
+
 def sum_terms(attn_out, grad_out, after):
-    parity, z, core = (lax.axis_index(axis) for axis in ("xl", "z", "core"))
-    terms = dot(attn_out, grad_out, 0, 0).astype(BF16).reshape(RING, 2, HD, D)
-
-    def part(which):
-        at = (0, which, (HD - HALF) * core, 0)
-        return lax.dynamic_slice(terms, at, (RING, 1, HALF, D)).reshape(RING, HALF, D)
-
-    total = add(part(parity), exchange(part(1 - parity), "xl"))
+    z = lax.axis_index("z")
+    own, other = terms(attn_out, grad_out)
+    total = add(own, exchange(other, "xl"))
     for apart in (1, 2, 4):
         mine = (z // apart) % 2
         halves = total.reshape(4 // apart, 2, HALF, D)

time: 144 us -> 144 us (level)
  waiting for transfers between devices: 22.8 us -> 20.1 us
  Pallas kernels: 11.7 us -> 13.9 us
  local copies, waits for them, and re-layouts: 2.71 us -> 1.19 us
  other arithmetic: 3.39 us -> 4.86 us
    pallas_call x0 -> x1, Pallas kernels: none -> 2.25 us  [terms(): pl.pallas_call(term_kernel, out_shape=(out, out), in_specs=[pl.BlockSpec(...]
    concatenate x2, other arithmetic: 0.05 us -> 1.64 us  [gather_weights(): blocks = jnp.concatenate([blocks, along_z(blocks, apart)], axis=0)]
    unnamed x12, local copies, waits for them, and re-layouts: 2.38 us -> 0.92 us
  transfers between devices with their start and end apart: 12 -> 12, of which waited for: 8 -> 6; matrix products, arithmetic and copies ran while one was open for 3% -> 4% of each run, Pallas kernels for 7% -> 9%
where the time goes in v3:
time: 144 us; the launch traced here: 143 us
  starting transfers between devices  57.6 us (40%)
  blocking collectives  42 us (29%)
  waiting for transfers between devices  20.1 us (14%)
  Pallas kernels  13.9 us (10%)
  other arithmetic  4.86 us (3%)
  matrix products  2.66 us (2%)
    all_to_all x1, blocking collectives, all_to_all(): return lax.all_to_all(x, axis, split_axis=0, concat_axis=0, tiled=True)  34 us
    ppermute x6, starting transfers between devices, along_z(): return lax.ppermute(x, 'z', [(i, i ^ apart) for i in range(RING)])  25.4 us
    all_to_all x3, starting transfers between devices, all_to_all(): return lax.all_to_all(x, axis, split_axis=0, concat_axis=0, tiled=True)  23.8 us
    ppermute x6, waiting for transfers between devices, along_z(): return lax.ppermute(x, 'z', [(i, i ^ apart) for i in range(RING)])  13.3 us
    ppermute x3, starting transfers between devices, exchange(): return lax.ppermute(x, axis, [(0, 1), (1, 0)])  8.39 us
    all_gather x3, blocking collectives, shards(): lax.all_gather(a, 'core', axis=0, tiled=True)  8.05 us
    pallas_call x1, Pallas kernels, attention(): pl.pallas_call(attention_kernel, out_shape=jax.ShapeDtypeStruct((HEADS, 3...  8.05 us
    all_to_all x3, waiting for transfers between devices, all_to_all(): return lax.all_to_all(x, axis, split_axis=0, concat_axis=0, tiled=True)  6.87 us
  transfers between devices with their start and end apart: 12, of which 6 were waited for; matrix products, arithmetic and copies ran while one was open for 4% of the time, Pallas kernels for 9%

profile of v3, /device:TPU:1, one launch (start us, length us, event | category | flops | bytes accessed | tf_op | source)
XLA Modules:
  0.0 143.4 jit_solution(16923967753953323179)
XLA Ops:
  0.6 0.0 copy-start
  0.7 0.9 copy-done
  1.6 11.5 %collective-permute-start = (bf16[40,1152]{1,0:T(8,128)(2,1)S(1)}, bf16[40,1152]{1,0:T(8,128)(2,1)S(1)}, u32[]{:S(2)}, u32[]{:S(2)}) collective-permute-start(bf16[40,1152]{1,0:T(8,128)(2,1)S(1)} %constant_dynamic-slice_fusion.1), channel_id=1, source_target_pairs={{0,128},{32,160},{64,192},{96,224},{128,0},{160,32},{192,64},{224,... | collective-permute-start | bytes 276488 | tf_op jit(solution)/shard_map/ppermute | solution.py:135
  13.0 3.0 %all_gather.9.g_ref = bf16[256,1152]{1,0:T(8,128)(2,1)S(1)} all-gather(bf16[128,1152]{1,0:T(8,128)(2,1)} %bitcast.84), channel_id=1, replica_groups=mesh['dp'=2,'z'=8,'xl'=2,'y'=8,'core'=2] {'core'}, dimensions={0}, use_global_device_ids=true | all-gather | bytes 884736 | tf_op jit(solution)/shard_map/all_gather | solution.py:262
  16.1 2.2 %all_gather.11.a_ref = bf16[256,1152]{1,0:T(8,128)(2,1)S(1)} all-gather(bf16[128,1152]{1,0:T(8,128)(2,1)S(1)} %bitcast.83), channel_id=1, replica_groups=mesh['dp'=2,'z'=8,'xl'=2,'y'=8,'core'=2] {'core'}, dimensions={0}, use_global_device_ids=true | all-gather | bytes 884736 | tf_op jit(solution)/shard_map/all_gather | solution.py:262
  18.3 0.1 fusion.2.place_ref
  18.4 2.3 %shard_map.96 = (bf16[8,40,1152]{2,1,0:T(8,128)(2,1)S(1)}, bf16[8,40,1152]{2,1,0:T(8,128)(2,1)}) custom-call(s32[2]{0:T(128)S(1)} %fusion.2.place_ref, bf16[256,1152]{1,0:T(8,128)(2,1)S(1)} %all_gather.11.a_ref, bf16[256,1152]{1,0:T(8,128)(2,1)S(1)} %all_gather.9.g_ref), custom_call_target="tpu_custom_call" | custom-call | flops 377487360 | bytes 3145728 | tf_op jit(solution)/shard_map/pallas_call | solution.py:202
  20.6 3.1 %collective-permute-start.5 = (bf16[8,40,1152]{2,1,0:T(8,128)(2,1)}, bf16[8,40,1152]{2,1,0:T(8,128)(2,1)}, u32[]{:S(2)}, u32[]{:S(2)}) collective-permute-start(bf16[8,40,1152]{2,1,0:T(8,128)(2,1)} %get-tuple-element.10), channel_id=1, source_target_pairs={{0,16},{16,0},{1,17},{17,1},{2,18},{18,2},{3,19},{19,3},{4,20},{20... | collective-permute-start | bytes 2211848 | tf_op jit(solution)/shard_map/ppermute | solution.py:127
  23.8 0.0 collective-permute-done
  23.8 0.7 pad_maximum_fusion.5
  24.5 4.0 %collective-permute-start.1 = (bf16[80,1152]{1,0:T(8,128)(2,1)}, bf16[80,1152]{1,0:T(8,128)(2,1)}, u32[]{:S(2)}, u32[]{:S(2)}) collective-permute-start(bf16[80,1152]{1,0:T(8,128)(2,1)} %pad_maximum_fusion.5), channel_id=1, source_target_pairs={{0,64},{32,96},{64,0},{96,32},{128,192},{160,224},{192,128},{224,1... | collective-permute-start | bytes 552968 | tf_op jit(solution)/shard_map/ppermute | solution.py:135
  28.5 2.2 %collective-permute-start.3 = (bf16[128,1152]{1,0:T(8,128)(2,1)S(1)}, bf16[128,1152]{1,0:T(8,128)(2,1)}, u32[]{:S(2)}, u32[]{:S(2)}) collective-permute-start(bf16[128,1152]{1,0:T(8,128)(2,1)S(1)} %bitcast.85), channel_id=1, source_target_pairs={{0,16},{16,0},{1,17},{17,1},{2,18},{18,2},{3,19},{19,3},{4,20},{20... | collective-permute-start | bytes 884744 | tf_op jit(solution)/shard_map/ppermute | solution.py:127
  30.7 1.2 shard_map.93
  31.9 8.3 %all-to-all-start = ((bf16[16,3,72,128]{3,2,1,0:T(8,128)(2,1)}), bf16[16,3,72,128]{3,2,1,0:T(8,128)(2,1)S(1)}, u32[]{:S(2)}, u32[]{:S(2)}) async-start(bf16[16,3,72,128]{3,2,1,0:T(8,128)(2,1)} %shard_map.93), calls=%async_computation | async-start | bytes 1769472 | tf_op jit(solution)/shard_map/all_to_all | solution.py:131
  40.2 0.1 pad_add_fusion.place_ref
  40.3 0.0 collective-permute-done.1
  40.3 1.0 pad_maximum_fusion.2
  41.3 3.1 %collective-permute-start.2 = (bf16[160,1152]{1,0:T(8,128)(2,1)S(1)}, bf16[160,1152]{1,0:T(8,128)(2,1)S(1)}, u32[]{:S(2)}, u32[]{:S(2)}) collective-permute-start(bf16[160,1152]{1,0:T(8,128)(2,1)S(1)} %pad_maximum_fusion.2), channel_id=1, source_target_pairs={{0,32},{32,0},{64,96},{96,64},{128,160},{160,128},{192,224},{224,1... | collective-permute-start | bytes 1105928 | tf_op jit(solution)/shard_map/ppermute | solution.py:135
  44.4 0.0 collective-permute-done.5
  44.4 1.3 add_convert_fusion
  45.7 2.2 %collective-permute-start.6 = (bf16[4,40,1152]{2,1,0:T(8,128)(2,1)S(1)}, bf16[4,40,1152]{2,1,0:T(8,128)(2,1)S(1)}, u32[]{:S(2)}, u32[]{:S(2)}) collective-permute-start(bf16[4,40,1152]{2,1,0:T(8,128)(2,1)S(1)} %dynamic-slice_bitcast_fusion), channel_id=1, source_target_pairs={{0,32},{32,0},{64,96},{96,64},{128,160},{160,128},{192,224},{224,1... | collective-permute-start | bytes 1105928 | tf_op jit(solution)/shard_map/ppermute | solution.py:135
  47.9 0.0 collective-permute-done.3
  47.9 2.8 %all_gather.10 = bf16[256,1152]{1,0:T(8,128)(2,1)S(1)} all-gather(bf16[128,1152]{1,0:T(8,128)(2,1)} %collective-permute-done.3), channel_id=1, replica_groups=mesh['dp'=2,'z'=8,'xl'=2,'y'=8,'core'=2] {'core'}, dimensions={0}, use_global_device_ids=true | all-gather | bytes 884736 | tf_op jit(solution)/shard_map/all_gather | solution.py:262
  50.8 2.4 %collective-permute-done.2 = bf16[160,1152]{1,0:T(8,128)(2,1)S(1)} collective-permute-done((bf16[160,1152]{1,0:T(8,128)(2,1)S(1)}, bf16[160,1152]{1,0:T(8,128)(2,1)S(1)}, u32[]{:S(2)}, u32[]{:S(2)}) %collective-permute-start.2) | collective-permute-done | bytes 368672 | tf_op jit(solution)/shard_map/ppermute | solution.py:135
  53.2 1.3 convolution_convert_fusion
  54.5 3.1 %collective-permute-start.4 = (bf16[320,256]{1,0:T(8,128)(2,1)S(1)}, bf16[320,256]{1,0:T(8,128)(2,1)S(1)}, u32[]{:S(2)}, u32[]{:S(2)}) collective-permute-start(bf16[320,256]{1,0:T(8,128)(2,1)S(1)} %convolution_convert_fusion), channel_id=1, source_target_pairs={{0,16},{16,0},{1,17},{17,1},{2,18},{18,2},{3,19},{19,3},{4,20},{20... | collective-permute-start | bytes 491528 | tf_op jit(solution)/shard_map/ppermute | solution.py:127
  57.6 3.4 %collective-permute-done.6 = bf16[4,40,1152]{2,1,0:T(8,128)(2,1)S(1)} collective-permute-done((bf16[4,40,1152]{2,1,0:T(8,128)(2,1)S(1)}, bf16[4,40,1152]{2,1,0:T(8,128)(2,1)S(1)}, u32[]{:S(2)}, u32[]{:S(2)}) %collective-permute-start.6) | collective-permute-done | bytes 368672 | tf_op jit(solution)/shard_map/ppermute | solution.py:135
  61.1 0.1 fusion
  61.2 2.2 %collective-permute-start.7 = (bf16[2,40,1152]{2,1,0:T(8,128)(2,1)S(1)}, bf16[2,40,1152]{2,1,0:T(8,128)(2,1)S(1)}, u32[]{:S(2)}, u32[]{:S(2)}) collective-permute-start(bf16[2,40,1152]{2,1,0:T(8,128)(2,1)S(1)} %dynamic-slice_bitcast_fusion.1), channel_id=1, source_target_pairs={{0,64},{32,96},{64,0},{96,32},{128,192},{160,224},{192,128},{224,1... | collective-permute-start | bytes 552968 | tf_op jit(solution)/shard_map/ppermute | solution.py:135
  63.4 1.3 convolution_convert_fusion.1
  64.7 0.1 all-to-all-done.after_ref.qkv_ref
  64.9 1.3 shard_map.94
  66.2 8.0 %all-to-all-start.1 = ((bf16[16,40,256]{2,1,0:T(8,128)(2,1)}), bf16[16,40,256]{2,1,0:T(8,128)(2,1)S(1)}, u32[]{:S(2)}, u32[]{:S(2)}) async-start(bf16[16,40,256]{2,1,0:T(8,128)(2,1)} %shard_map.94), calls=%async_computation.1 | async-start | bytes 655360 | tf_op jit(solution)/shard_map/all_to_all | solution.py:131
  74.2 0.0 collective-permute-done.7
  74.2 0.1 fusion.1
  74.3 2.5 %collective-permute-start.8 = (bf16[1,40,1152]{2,1,0:T(8,128)(2,1)S(1)}, bf16[1,40,1152]{2,1,0:T(8,128)(2,1)S(1)}, u32[]{:S(2)}, u32[]{:S(2)}) collective-permute-start(bf16[1,40,1152]{2,1,0:T(8,128)(2,1)S(1)} %get-tuple-element.28), channel_id=1, source_target_pairs={{0,128},{32,160},{64,192},{96,224},{128,0},{160,32},{192,64},{224,... | collective-permute-start | bytes 276488 | tf_op jit(solution)/shard_map/ppermute | solution.py:135
  76.8 7.4 %collective-permute-done.8 = bf16[1,40,1152]{2,1,0:T(8,128)(2,1)S(1)} collective-permute-done((bf16[1,40,1152]{2,1,0:T(8,128)(2,1)S(1)}, bf16[1,40,1152]{2,1,0:T(8,128)(2,1)S(1)}, u32[]{:S(2)}, u32[]{:S(2)}) %collective-permute-start.8) | collective-permute-done | bytes 92192 | tf_op jit(solution)/shard_map/ppermute | solution.py:135
  84.2 3.1 %all-to-all-done.1.g_ref.after_ref = bf16[16,40,256]{2,1,0:T(8,128)(2,1)S(1)} async-done(((bf16[16,40,256]{2,1,0:T(8,128)(2,1)}), bf16[16,40,256]{2,1,0:T(8,128)(2,1)S(1)}, u32[]{:S(2)}, u32[]{:S(2)}) %all-to-all-start.1) | async-done | bytes 327712 | tf_op jit(solution)/shard_map/all_to_all | solution.py:131
  87.3 0.7 pad_maximum_fusion.4
  88.0 7.5 %all-to-all-start.2 = ((bf16[32,24,128]{2,1,0:T(8,128)(2,1)}), bf16[32,24,128]{2,1,0:T(8,128)(2,1)S(1)}, u32[]{:S(2)}, u32[]{:S(2)}) async-start(bf16[32,24,128]{2,1,0:T(8,128)(2,1)} %pad_maximum_fusion.4), calls=%async_computation.2 | async-start | bytes 393216 | tf_op jit(solution)/shard_map/all_to_all | solution.py:131
  95.5 8.1 %shard_map.95 = bf16[16,3,72,128]{3,2,1,0:T(8,128)(2,1)S(1)} custom-call(bf16[16,3,72,128]{3,2,1,0:T(8,128)(2,1)S(1)} %all-to-all-done.after_ref.qkv_ref, bf16[16,40,256]{2,1,0:T(8,128)(2,1)S(1)} %all-to-all-done.1.g_ref.after_ref), custom_call_target="tpu_custom_call" | custom-call | flops 5368709120 | bytes 3145728 | tf_op jit(solution)/shard_map/pallas_call | solution.py:113
  103.5 3.6 %all-to-all-done.2 = bf16[32,24,128]{2,1,0:T(8,128)(2,1)S(1)} async-done(((bf16[32,24,128]{2,1,0:T(8,128)(2,1)}), bf16[32,24,128]{2,1,0:T(8,128)(2,1)S(1)}, u32[]{:S(2)}, u32[]{:S(2)}) %all-to-all-start.2) | async-done | bytes 196640 | tf_op jit(solution)/shard_map/all_to_all | solution.py:131
  107.3 0.1 pad_maximum_fusion
  107.3 34.0 %all_to_all.20 = bf16[16,264,128]{2,1,0:T(8,128)(2,1)S(1)} all-to-all(bf16[16,264,128]{2,1,0:T(8,128)(2,1)S(1)} %pad_maximum_fusion), channel_id=1, replica_groups=mesh['dp'=2,'z'=8,'xl'=2,'y'=8,'core'=2] {'y','core'}, dimensions={0} | all-to-all | bytes 2162688 | tf_op jit(solution)/shard_map/all_to_all | solution.py:131
  141.4 0.1 convert_bitcast_fusion.1
  141.5 0.1 slice.22
  141.6 1.1 shard_map.98
  142.6 0.7 pad_maximum_fusion.3
  (24 shorter events, 0.3 us)
Async XLA Ops:
  0.6 0.9 copy-start
  0.6 15.4 %copy-start.4 = (bf16[2,1,2,32,1152]{4,3,2,1,0:T(8,128)(2,1)S(1)}, bf16[2,1,2,32,1152]{4,3,2,1,0:T(8,128)(2,1)}, u32[]{:S(2)}) copy-start(bf16[2,1,2,32,1152]{4,3,2,1,0:T(8,128)(2,1)} %param.10) | copy-start | bytes 884740
  1.6 22.2 %collective-permute-start = (bf16[40,1152]{1,0:T(8,128)(2,1)S(1)}, bf16[40,1152]{1,0:T(8,128)(2,1)S(1)}, u32[]{:S(2)}, u32[]{:S(2)}) collective-permute-start(bf16[40,1152]{1,0:T(8,128)(2,1)S(1)} %constant_dynamic-slice_fusion.1), channel_id=1, source_target_pairs={{0,128},{32,160},{64,192},{96,224},{128,0},{160,32},{192,64},{224,... | collective-permute-start | bytes 276488 | tf_op jit(solution)/shard_map/ppermute | solution.py:135
  18.3 10.2 %copy-start.5 = (bf16[2,1,2,32,1152]{4,3,2,1,0:T(8,128)(2,1)S(1)}, bf16[2,1,2,32,1152]{4,3,2,1,0:T(8,128)(2,1)}, u32[]{:S(2)}) copy-start(bf16[2,1,2,32,1152]{4,3,2,1,0:T(8,128)(2,1)} %param.9) | copy-start | bytes 884740
  18.3 12.4 %copy-start.1 = (bf16[2,1,2,32,1152]{4,3,2,1,0:T(8,128)(2,1)S(1)}, bf16[2,1,2,32,1152]{4,3,2,1,0:T(8,128)(2,1)}, u32[]{:S(2)}) copy-start(bf16[2,1,2,32,1152]{4,3,2,1,0:T(8,128)(2,1)} %param.6) | copy-start | bytes 884740
  18.3 12.4 %copy-start.2 = (bf16[2,1,2,32,1152]{4,3,2,1,0:T(8,128)(2,1)S(1)}, bf16[2,1,2,32,1152]{4,3,2,1,0:T(8,128)(2,1)}, u32[]{:S(2)}) copy-start(bf16[2,1,2,32,1152]{4,3,2,1,0:T(8,128)(2,1)} %param.7) | copy-start | bytes 884740
  18.3 12.4 %copy-start.3 = (bf16[2,1,2,32,1152]{4,3,2,1,0:T(8,128)(2,1)S(1)}, bf16[2,1,2,32,1152]{4,3,2,1,0:T(8,128)(2,1)}, u32[]{:S(2)}) copy-start(bf16[2,1,2,32,1152]{4,3,2,1,0:T(8,128)(2,1)} %param.8) | copy-start | bytes 884740
  20.6 23.7 %collective-permute-start.5 = (bf16[8,40,1152]{2,1,0:T(8,128)(2,1)}, bf16[8,40,1152]{2,1,0:T(8,128)(2,1)}, u32[]{:S(2)}, u32[]{:S(2)}) collective-permute-start(bf16[8,40,1152]{2,1,0:T(8,128)(2,1)} %get-tuple-element.10), channel_id=1, source_target_pairs={{0,16},{16,0},{1,17},{17,1},{2,18},{18,2},{3,19},{19,3},{4,20},{20... | collective-permute-start | bytes 2211848 | tf_op jit(solution)/shard_map/ppermute | solution.py:127
  24.5 15.9 %collective-permute-start.1 = (bf16[80,1152]{1,0:T(8,128)(2,1)}, bf16[80,1152]{1,0:T(8,128)(2,1)}, u32[]{:S(2)}, u32[]{:S(2)}) collective-permute-start(bf16[80,1152]{1,0:T(8,128)(2,1)} %pad_maximum_fusion.5), channel_id=1, source_target_pairs={{0,64},{32,96},{64,0},{96,32},{128,192},{160,224},{192,128},{224,1... | collective-permute-start | bytes 552968 | tf_op jit(solution)/shard_map/ppermute | solution.py:135
  28.5 19.5 %collective-permute-start.3 = (bf16[128,1152]{1,0:T(8,128)(2,1)S(1)}, bf16[128,1152]{1,0:T(8,128)(2,1)}, u32[]{:S(2)}, u32[]{:S(2)}) collective-permute-start(bf16[128,1152]{1,0:T(8,128)(2,1)S(1)} %bitcast.85), channel_id=1, source_target_pairs={{0,16},{16,0},{1,17},{17,1},{2,18},{18,2},{3,19},{19,3},{4,20},{20... | collective-permute-start | bytes 884744 | tf_op jit(solution)/shard_map/ppermute | solution.py:127
  31.9 33.0 %all-to-all-start = ((bf16[16,3,72,128]{3,2,1,0:T(8,128)(2,1)}), bf16[16,3,72,128]{3,2,1,0:T(8,128)(2,1)S(1)}, u32[]{:S(2)}, u32[]{:S(2)}) async-start(bf16[16,3,72,128]{3,2,1,0:T(8,128)(2,1)} %shard_map.93), calls=%async_computation | async-start | bytes 1769472 | tf_op jit(solution)/shard_map/all_to_all | solution.py:131
  41.3 11.9 %collective-permute-start.2 = (bf16[160,1152]{1,0:T(8,128)(2,1)S(1)}, bf16[160,1152]{1,0:T(8,128)(2,1)S(1)}, u32[]{:S(2)}, u32[]{:S(2)}) collective-permute-start(bf16[160,1152]{1,0:T(8,128)(2,1)S(1)} %pad_maximum_fusion.2), channel_id=1, source_target_pairs={{0,32},{32,0},{64,96},{96,64},{128,160},{160,128},{192,224},{224,1... | collective-permute-start | bytes 1105928 | tf_op jit(solution)/shard_map/ppermute | solution.py:135
  45.7 15.3 %collective-permute-start.6 = (bf16[4,40,1152]{2,1,0:T(8,128)(2,1)S(1)}, bf16[4,40,1152]{2,1,0:T(8,128)(2,1)S(1)}, u32[]{:S(2)}, u32[]{:S(2)}) collective-permute-start(bf16[4,40,1152]{2,1,0:T(8,128)(2,1)S(1)} %dynamic-slice_bitcast_fusion), channel_id=1, source_target_pairs={{0,32},{32,0},{64,96},{96,64},{128,160},{160,128},{192,224},{224,1... | collective-permute-start | bytes 1105928 | tf_op jit(solution)/shard_map/ppermute | solution.py:135
  54.5 10.2 %collective-permute-start.4 = (bf16[320,256]{1,0:T(8,128)(2,1)S(1)}, bf16[320,256]{1,0:T(8,128)(2,1)S(1)}, u32[]{:S(2)}, u32[]{:S(2)}) collective-permute-start(bf16[320,256]{1,0:T(8,128)(2,1)S(1)} %convolution_convert_fusion), channel_id=1, source_target_pairs={{0,16},{16,0},{1,17},{17,1},{2,18},{18,2},{3,19},{19,3},{4,20},{20... | collective-permute-start | bytes 491528 | tf_op jit(solution)/shard_map/ppermute | solution.py:127
  61.2 13.0 %collective-permute-start.7 = (bf16[2,40,1152]{2,1,0:T(8,128)(2,1)S(1)}, bf16[2,40,1152]{2,1,0:T(8,128)(2,1)S(1)}, u32[]{:S(2)}, u32[]{:S(2)}) collective-permute-start(bf16[2,40,1152]{2,1,0:T(8,128)(2,1)S(1)} %dynamic-slice_bitcast_fusion.1), channel_id=1, source_target_pairs={{0,64},{32,96},{64,0},{96,32},{128,192},{160,224},{192,128},{224,1... | collective-permute-start | bytes 552968 | tf_op jit(solution)/shard_map/ppermute | solution.py:135
  66.2 21.1 %all-to-all-start.1 = ((bf16[16,40,256]{2,1,0:T(8,128)(2,1)}), bf16[16,40,256]{2,1,0:T(8,128)(2,1)S(1)}, u32[]{:S(2)}, u32[]{:S(2)}) async-start(bf16[16,40,256]{2,1,0:T(8,128)(2,1)} %shard_map.94), calls=%async_computation.1 | async-start | bytes 655360 | tf_op jit(solution)/shard_map/all_to_all | solution.py:131
  74.3 9.9 %collective-permute-start.8 = (bf16[1,40,1152]{2,1,0:T(8,128)(2,1)S(1)}, bf16[1,40,1152]{2,1,0:T(8,128)(2,1)S(1)}, u32[]{:S(2)}, u32[]{:S(2)}) collective-permute-start(bf16[1,40,1152]{2,1,0:T(8,128)(2,1)S(1)} %get-tuple-element.28), channel_id=1, source_target_pairs={{0,128},{32,160},{64,192},{96,224},{128,0},{160,32},{192,64},{224,... | collective-permute-start | bytes 276488 | tf_op jit(solution)/shard_map/ppermute | solution.py:135
  88.0 19.2 %all-to-all-start.2 = ((bf16[32,24,128]{2,1,0:T(8,128)(2,1)}), bf16[32,24,128]{2,1,0:T(8,128)(2,1)S(1)}, u32[]{:S(2)}, u32[]{:S(2)}) async-start(bf16[32,24,128]{2,1,0:T(8,128)(2,1)} %pad_maximum_fusion.4), calls=%async_computation.2 | async-start | bytes 393216 | tf_op jit(solution)/shard_map/all_to_all | solution.py:131

commit v4 on v3

--- a/solution.py
+++ b/solution.py
@@ -204,7 +204,7 @@
         out_shape=(out, out),
         in_specs=[pl.BlockSpec(memory_space=pltpu.SMEM), vmem, vmem],
         scratch_shapes=[pltpu.VMEM((D, 2 * TOKENS), F32)],
-        compiler_params=pltpu.CompilerParams(vmem_limit_bytes=24 * 2**20),
+        compiler_params=pltpu.CompilerParams(vmem_limit_bytes=12 * 2**20),
         cost_estimate=pl.CostEstimate(
             flops=4 * RING * HALF * D * 2 * TOKENS, bytes_accessed=3 * 2**20, transcendentals=0
         ),

time: 144 us -> 144 us (level)
  no operation moved by 1% of the time
where the time goes in v4:
time: 144 us; the launch traced here: 143 us
  starting transfers between devices  57.6 us (40%)
  blocking collectives  42 us (29%)
  waiting for transfers between devices  20.1 us (14%)
  Pallas kernels  13.9 us (10%)
  other arithmetic  4.86 us (3%)
  matrix products  2.66 us (2%)
    all_to_all x1, blocking collectives, all_to_all(): return lax.all_to_all(x, axis, split_axis=0, concat_axis=0, tiled=True)  34 us
    ppermute x6, starting transfers between devices, along_z(): return lax.ppermute(x, 'z', [(i, i ^ apart) for i in range(RING)])  25.4 us
    all_to_all x3, starting transfers between devices, all_to_all(): return lax.all_to_all(x, axis, split_axis=0, concat_axis=0, tiled=True)  23.8 us
    ppermute x6, waiting for transfers between devices, along_z(): return lax.ppermute(x, 'z', [(i, i ^ apart) for i in range(RING)])  13.3 us
    ppermute x3, starting transfers between devices, exchange(): return lax.ppermute(x, axis, [(0, 1), (1, 0)])  8.39 us
    all_gather x3, blocking collectives, shards(): lax.all_gather(a, 'core', axis=0, tiled=True)  8.05 us
    pallas_call x1, Pallas kernels, attention(): pl.pallas_call(attention_kernel, out_shape=jax.ShapeDtypeStruct((HEADS, 3...  8.05 us
    all_to_all x3, waiting for transfers between devices, all_to_all(): return lax.all_to_all(x, axis, split_axis=0, concat_axis=0, tiled=True)  6.87 us
  transfers between devices with their start and end apart: 12, of which 6 were waited for; matrix products, arithmetic and copies ran while one was open for 4% of the time, Pallas kernels for 9%

profile of v4, /device:TPU:1, one launch (start us, length us, event | category | flops | bytes accessed | tf_op | source)
XLA Modules:
  0.0 143.4 jit_solution(13701376870263852791)
XLA Ops:
  0.6 0.0 copy-start
  0.7 0.9 copy-done
  1.6 11.5 %collective-permute-start = (bf16[40,1152]{1,0:T(8,128)(2,1)S(1)}, bf16[40,1152]{1,0:T(8,128)(2,1)S(1)}, u32[]{:S(2)}, u32[]{:S(2)}) collective-permute-start(bf16[40,1152]{1,0:T(8,128)(2,1)S(1)} %constant_dynamic-slice_fusion.1), channel_id=1, source_target_pairs={{0,128},{32,160},{64,192},{96,224},{128,0},{160,32},{192,64},{224,... | collective-permute-start | bytes 276488 | tf_op jit(solution)/shard_map/ppermute | solution.py:135
  13.0 3.0 %all_gather.9.g_ref = bf16[256,1152]{1,0:T(8,128)(2,1)S(1)} all-gather(bf16[128,1152]{1,0:T(8,128)(2,1)} %bitcast.84), channel_id=1, replica_groups=mesh['dp'=2,'z'=8,'xl'=2,'y'=8,'core'=2] {'core'}, dimensions={0}, use_global_device_ids=true | all-gather | bytes 884736 | tf_op jit(solution)/shard_map/all_gather | solution.py:262
  16.1 2.2 %all_gather.11.a_ref = bf16[256,1152]{1,0:T(8,128)(2,1)S(1)} all-gather(bf16[128,1152]{1,0:T(8,128)(2,1)S(1)} %bitcast.83), channel_id=1, replica_groups=mesh['dp'=2,'z'=8,'xl'=2,'y'=8,'core'=2] {'core'}, dimensions={0}, use_global_device_ids=true | all-gather | bytes 884736 | tf_op jit(solution)/shard_map/all_gather | solution.py:262
  18.3 0.1 fusion.2.place_ref
  18.4 2.3 %shard_map.96 = (bf16[8,40,1152]{2,1,0:T(8,128)(2,1)S(1)}, bf16[8,40,1152]{2,1,0:T(8,128)(2,1)}) custom-call(s32[2]{0:T(128)S(1)} %fusion.2.place_ref, bf16[256,1152]{1,0:T(8,128)(2,1)S(1)} %all_gather.11.a_ref, bf16[256,1152]{1,0:T(8,128)(2,1)S(1)} %all_gather.9.g_ref), custom_call_target="tpu_custom_call" | custom-call | flops 377487360 | bytes 3145728 | tf_op jit(solution)/shard_map/pallas_call | solution.py:202
  20.6 3.1 %collective-permute-start.5 = (bf16[8,40,1152]{2,1,0:T(8,128)(2,1)}, bf16[8,40,1152]{2,1,0:T(8,128)(2,1)}, u32[]{:S(2)}, u32[]{:S(2)}) collective-permute-start(bf16[8,40,1152]{2,1,0:T(8,128)(2,1)} %get-tuple-element.10), channel_id=1, source_target_pairs={{0,16},{16,0},{1,17},{17,1},{2,18},{18,2},{3,19},{19,3},{4,20},{20... | collective-permute-start | bytes 2211848 | tf_op jit(solution)/shard_map/ppermute | solution.py:127
  23.8 0.0 collective-permute-done
  23.8 0.7 pad_maximum_fusion.5
  24.5 4.0 %collective-permute-start.1 = (bf16[80,1152]{1,0:T(8,128)(2,1)}, bf16[80,1152]{1,0:T(8,128)(2,1)}, u32[]{:S(2)}, u32[]{:S(2)}) collective-permute-start(bf16[80,1152]{1,0:T(8,128)(2,1)} %pad_maximum_fusion.5), channel_id=1, source_target_pairs={{0,64},{32,96},{64,0},{96,32},{128,192},{160,224},{192,128},{224,1... | collective-permute-start | bytes 552968 | tf_op jit(solution)/shard_map/ppermute | solution.py:135
  28.5 2.2 %collective-permute-start.3 = (bf16[128,1152]{1,0:T(8,128)(2,1)S(1)}, bf16[128,1152]{1,0:T(8,128)(2,1)}, u32[]{:S(2)}, u32[]{:S(2)}) collective-permute-start(bf16[128,1152]{1,0:T(8,128)(2,1)S(1)} %bitcast.85), channel_id=1, source_target_pairs={{0,16},{16,0},{1,17},{17,1},{2,18},{18,2},{3,19},{19,3},{4,20},{20... | collective-permute-start | bytes 884744 | tf_op jit(solution)/shard_map/ppermute | solution.py:127
  30.7 1.2 shard_map.93
  31.9 8.3 %all-to-all-start = ((bf16[16,3,72,128]{3,2,1,0:T(8,128)(2,1)}), bf16[16,3,72,128]{3,2,1,0:T(8,128)(2,1)S(1)}, u32[]{:S(2)}, u32[]{:S(2)}) async-start(bf16[16,3,72,128]{3,2,1,0:T(8,128)(2,1)} %shard_map.93), calls=%async_computation | async-start | bytes 1769472 | tf_op jit(solution)/shard_map/all_to_all | solution.py:131
  40.2 0.1 pad_add_fusion.place_ref
  40.3 0.0 collective-permute-done.1
  40.3 1.0 pad_maximum_fusion.2
  41.3 3.1 %collective-permute-start.2 = (bf16[160,1152]{1,0:T(8,128)(2,1)S(1)}, bf16[160,1152]{1,0:T(8,128)(2,1)S(1)}, u32[]{:S(2)}, u32[]{:S(2)}) collective-permute-start(bf16[160,1152]{1,0:T(8,128)(2,1)S(1)} %pad_maximum_fusion.2), channel_id=1, source_target_pairs={{0,32},{32,0},{64,96},{96,64},{128,160},{160,128},{192,224},{224,1... | collective-permute-start | bytes 1105928 | tf_op jit(solution)/shard_map/ppermute | solution.py:135
  44.4 0.0 collective-permute-done.5
  44.4 1.3 add_convert_fusion
  45.7 2.2 %collective-permute-start.6 = (bf16[4,40,1152]{2,1,0:T(8,128)(2,1)S(1)}, bf16[4,40,1152]{2,1,0:T(8,128)(2,1)S(1)}, u32[]{:S(2)}, u32[]{:S(2)}) collective-permute-start(bf16[4,40,1152]{2,1,0:T(8,128)(2,1)S(1)} %dynamic-slice_bitcast_fusion), channel_id=1, source_target_pairs={{0,32},{32,0},{64,96},{96,64},{128,160},{160,128},{192,224},{224,1... | collective-permute-start | bytes 1105928 | tf_op jit(solution)/shard_map/ppermute | solution.py:135
  47.9 0.0 collective-permute-done.3
  47.9 2.8 %all_gather.10 = bf16[256,1152]{1,0:T(8,128)(2,1)S(1)} all-gather(bf16[128,1152]{1,0:T(8,128)(2,1)} %collective-permute-done.3), channel_id=1, replica_groups=mesh['dp'=2,'z'=8,'xl'=2,'y'=8,'core'=2] {'core'}, dimensions={0}, use_global_device_ids=true | all-gather | bytes 884736 | tf_op jit(solution)/shard_map/all_gather | solution.py:262
  50.8 2.4 %collective-permute-done.2 = bf16[160,1152]{1,0:T(8,128)(2,1)S(1)} collective-permute-done((bf16[160,1152]{1,0:T(8,128)(2,1)S(1)}, bf16[160,1152]{1,0:T(8,128)(2,1)S(1)}, u32[]{:S(2)}, u32[]{:S(2)}) %collective-permute-start.2) | collective-permute-done | bytes 368672 | tf_op jit(solution)/shard_map/ppermute | solution.py:135
  53.2 1.3 convolution_convert_fusion
  54.5 3.1 %collective-permute-start.4 = (bf16[320,256]{1,0:T(8,128)(2,1)S(1)}, bf16[320,256]{1,0:T(8,128)(2,1)S(1)}, u32[]{:S(2)}, u32[]{:S(2)}) collective-permute-start(bf16[320,256]{1,0:T(8,128)(2,1)S(1)} %convolution_convert_fusion), channel_id=1, source_target_pairs={{0,16},{16,0},{1,17},{17,1},{2,18},{18,2},{3,19},{19,3},{4,20},{20... | collective-permute-start | bytes 491528 | tf_op jit(solution)/shard_map/ppermute | solution.py:127
  57.6 3.4 %collective-permute-done.6 = bf16[4,40,1152]{2,1,0:T(8,128)(2,1)S(1)} collective-permute-done((bf16[4,40,1152]{2,1,0:T(8,128)(2,1)S(1)}, bf16[4,40,1152]{2,1,0:T(8,128)(2,1)S(1)}, u32[]{:S(2)}, u32[]{:S(2)}) %collective-permute-start.6) | collective-permute-done | bytes 368672 | tf_op jit(solution)/shard_map/ppermute | solution.py:135
  61.1 0.1 fusion
  61.2 2.2 %collective-permute-start.7 = (bf16[2,40,1152]{2,1,0:T(8,128)(2,1)S(1)}, bf16[2,40,1152]{2,1,0:T(8,128)(2,1)S(1)}, u32[]{:S(2)}, u32[]{:S(2)}) collective-permute-start(bf16[2,40,1152]{2,1,0:T(8,128)(2,1)S(1)} %dynamic-slice_bitcast_fusion.1), channel_id=1, source_target_pairs={{0,64},{32,96},{64,0},{96,32},{128,192},{160,224},{192,128},{224,1... | collective-permute-start | bytes 552968 | tf_op jit(solution)/shard_map/ppermute | solution.py:135
  63.4 1.3 convolution_convert_fusion.1
  64.7 0.0 collective-permute-done.4
  64.7 0.1 all-to-all-done.after_ref.qkv_ref
  64.9 1.3 shard_map.94
  66.2 8.0 %all-to-all-start.1 = ((bf16[16,40,256]{2,1,0:T(8,128)(2,1)}), bf16[16,40,256]{2,1,0:T(8,128)(2,1)S(1)}, u32[]{:S(2)}, u32[]{:S(2)}) async-start(bf16[16,40,256]{2,1,0:T(8,128)(2,1)} %shard_map.94), calls=%async_computation.1 | async-start | bytes 655360 | tf_op jit(solution)/shard_map/all_to_all | solution.py:131
  74.2 0.1 fusion.1
  74.3 2.5 %collective-permute-start.8 = (bf16[1,40,1152]{2,1,0:T(8,128)(2,1)S(1)}, bf16[1,40,1152]{2,1,0:T(8,128)(2,1)S(1)}, u32[]{:S(2)}, u32[]{:S(2)}) collective-permute-start(bf16[1,40,1152]{2,1,0:T(8,128)(2,1)S(1)} %get-tuple-element.28), channel_id=1, source_target_pairs={{0,128},{32,160},{64,192},{96,224},{128,0},{160,32},{192,64},{224,... | collective-permute-start | bytes 276488 | tf_op jit(solution)/shard_map/ppermute | solution.py:135
  76.8 7.4 %collective-permute-done.8 = bf16[1,40,1152]{2,1,0:T(8,128)(2,1)S(1)} collective-permute-done((bf16[1,40,1152]{2,1,0:T(8,128)(2,1)S(1)}, bf16[1,40,1152]{2,1,0:T(8,128)(2,1)S(1)}, u32[]{:S(2)}, u32[]{:S(2)}) %collective-permute-start.8) | collective-permute-done | bytes 92192 | tf_op jit(solution)/shard_map/ppermute | solution.py:135
  84.2 3.1 %all-to-all-done.1.g_ref.after_ref = bf16[16,40,256]{2,1,0:T(8,128)(2,1)S(1)} async-done(((bf16[16,40,256]{2,1,0:T(8,128)(2,1)}), bf16[16,40,256]{2,1,0:T(8,128)(2,1)S(1)}, u32[]{:S(2)}, u32[]{:S(2)}) %all-to-all-start.1) | async-done | bytes 327712 | tf_op jit(solution)/shard_map/all_to_all | solution.py:131
  87.3 0.7 pad_maximum_fusion.4
  88.0 7.5 %all-to-all-start.2 = ((bf16[32,24,128]{2,1,0:T(8,128)(2,1)}), bf16[32,24,128]{2,1,0:T(8,128)(2,1)S(1)}, u32[]{:S(2)}, u32[]{:S(2)}) async-start(bf16[32,24,128]{2,1,0:T(8,128)(2,1)} %pad_maximum_fusion.4), calls=%async_computation.2 | async-start | bytes 393216 | tf_op jit(solution)/shard_map/all_to_all | solution.py:131
  95.5 8.1 %shard_map.95 = bf16[16,3,72,128]{3,2,1,0:T(8,128)(2,1)S(1)} custom-call(bf16[16,3,72,128]{3,2,1,0:T(8,128)(2,1)S(1)} %all-to-all-done.after_ref.qkv_ref, bf16[16,40,256]{2,1,0:T(8,128)(2,1)S(1)} %all-to-all-done.1.g_ref.after_ref), custom_call_target="tpu_custom_call" | custom-call | flops 5368709120 | bytes 3145728 | tf_op jit(solution)/shard_map/pallas_call | solution.py:113
  103.5 3.6 %all-to-all-done.2 = bf16[32,24,128]{2,1,0:T(8,128)(2,1)S(1)} async-done(((bf16[32,24,128]{2,1,0:T(8,128)(2,1)}), bf16[32,24,128]{2,1,0:T(8,128)(2,1)S(1)}, u32[]{:S(2)}, u32[]{:S(2)}) %all-to-all-start.2) | async-done | bytes 196640 | tf_op jit(solution)/shard_map/all_to_all | solution.py:131
  107.3 0.1 pad_maximum_fusion
  107.3 34.0 %all_to_all.20 = bf16[16,264,128]{2,1,0:T(8,128)(2,1)S(1)} all-to-all(bf16[16,264,128]{2,1,0:T(8,128)(2,1)S(1)} %pad_maximum_fusion), channel_id=1, replica_groups=mesh['dp'=2,'z'=8,'xl'=2,'y'=8,'core'=2] {'y','core'}, dimensions={0} | all-to-all | bytes 2162688 | tf_op jit(solution)/shard_map/all_to_all | solution.py:131
  141.4 0.1 convert_bitcast_fusion.1
  141.5 0.1 slice.22
  141.6 1.1 shard_map.98
  142.6 0.7 pad_maximum_fusion.3
  (24 shorter events, 0.3 us)
Async XLA Ops:
  0.6 0.9 copy-start
  0.6 15.4 %copy-start.4 = (bf16[2,1,2,32,1152]{4,3,2,1,0:T(8,128)(2,1)S(1)}, bf16[2,1,2,32,1152]{4,3,2,1,0:T(8,128)(2,1)}, u32[]{:S(2)}) copy-start(bf16[2,1,2,32,1152]{4,3,2,1,0:T(8,128)(2,1)} %param.10) | copy-start | bytes 884740
  1.6 22.2 %collective-permute-start = (bf16[40,1152]{1,0:T(8,128)(2,1)S(1)}, bf16[40,1152]{1,0:T(8,128)(2,1)S(1)}, u32[]{:S(2)}, u32[]{:S(2)}) collective-permute-start(bf16[40,1152]{1,0:T(8,128)(2,1)S(1)} %constant_dynamic-slice_fusion.1), channel_id=1, source_target_pairs={{0,128},{32,160},{64,192},{96,224},{128,0},{160,32},{192,64},{224,... | collective-permute-start | bytes 276488 | tf_op jit(solution)/shard_map/ppermute | solution.py:135
  18.3 10.2 %copy-start.5 = (bf16[2,1,2,32,1152]{4,3,2,1,0:T(8,128)(2,1)S(1)}, bf16[2,1,2,32,1152]{4,3,2,1,0:T(8,128)(2,1)}, u32[]{:S(2)}) copy-start(bf16[2,1,2,32,1152]{4,3,2,1,0:T(8,128)(2,1)} %param.9) | copy-start | bytes 884740
  18.3 12.4 %copy-start.1 = (bf16[2,1,2,32,1152]{4,3,2,1,0:T(8,128)(2,1)S(1)}, bf16[2,1,2,32,1152]{4,3,2,1,0:T(8,128)(2,1)}, u32[]{:S(2)}) copy-start(bf16[2,1,2,32,1152]{4,3,2,1,0:T(8,128)(2,1)} %param.6) | copy-start | bytes 884740
  18.3 12.4 %copy-start.2 = (bf16[2,1,2,32,1152]{4,3,2,1,0:T(8,128)(2,1)S(1)}, bf16[2,1,2,32,1152]{4,3,2,1,0:T(8,128)(2,1)}, u32[]{:S(2)}) copy-start(bf16[2,1,2,32,1152]{4,3,2,1,0:T(8,128)(2,1)} %param.7) | copy-start | bytes 884740
  18.3 12.4 %copy-start.3 = (bf16[2,1,2,32,1152]{4,3,2,1,0:T(8,128)(2,1)S(1)}, bf16[2,1,2,32,1152]{4,3,2,1,0:T(8,128)(2,1)}, u32[]{:S(2)}) copy-start(bf16[2,1,2,32,1152]{4,3,2,1,0:T(8,128)(2,1)} %param.8) | copy-start | bytes 884740
  20.6 23.7 %collective-permute-start.5 = (bf16[8,40,1152]{2,1,0:T(8,128)(2,1)}, bf16[8,40,1152]{2,1,0:T(8,128)(2,1)}, u32[]{:S(2)}, u32[]{:S(2)}) collective-permute-start(bf16[8,40,1152]{2,1,0:T(8,128)(2,1)} %get-tuple-element.10), channel_id=1, source_target_pairs={{0,16},{16,0},{1,17},{17,1},{2,18},{18,2},{3,19},{19,3},{4,20},{20... | collective-permute-start | bytes 2211848 | tf_op jit(solution)/shard_map/ppermute | solution.py:127
  24.5 15.9 %collective-permute-start.1 = (bf16[80,1152]{1,0:T(8,128)(2,1)}, bf16[80,1152]{1,0:T(8,128)(2,1)}, u32[]{:S(2)}, u32[]{:S(2)}) collective-permute-start(bf16[80,1152]{1,0:T(8,128)(2,1)} %pad_maximum_fusion.5), channel_id=1, source_target_pairs={{0,64},{32,96},{64,0},{96,32},{128,192},{160,224},{192,128},{224,1... | collective-permute-start | bytes 552968 | tf_op jit(solution)/shard_map/ppermute | solution.py:135
  28.5 19.5 %collective-permute-start.3 = (bf16[128,1152]{1,0:T(8,128)(2,1)S(1)}, bf16[128,1152]{1,0:T(8,128)(2,1)}, u32[]{:S(2)}, u32[]{:S(2)}) collective-permute-start(bf16[128,1152]{1,0:T(8,128)(2,1)S(1)} %bitcast.85), channel_id=1, source_target_pairs={{0,16},{16,0},{1,17},{17,1},{2,18},{18,2},{3,19},{19,3},{4,20},{20... | collective-permute-start | bytes 884744 | tf_op jit(solution)/shard_map/ppermute | solution.py:127
  31.9 33.0 %all-to-all-start = ((bf16[16,3,72,128]{3,2,1,0:T(8,128)(2,1)}), bf16[16,3,72,128]{3,2,1,0:T(8,128)(2,1)S(1)}, u32[]{:S(2)}, u32[]{:S(2)}) async-start(bf16[16,3,72,128]{3,2,1,0:T(8,128)(2,1)} %shard_map.93), calls=%async_computation | async-start | bytes 1769472 | tf_op jit(solution)/shard_map/all_to_all | solution.py:131
  41.3 11.9 %collective-permute-start.2 = (bf16[160,1152]{1,0:T(8,128)(2,1)S(1)}, bf16[160,1152]{1,0:T(8,128)(2,1)S(1)}, u32[]{:S(2)}, u32[]{:S(2)}) collective-permute-start(bf16[160,1152]{1,0:T(8,128)(2,1)S(1)} %pad_maximum_fusion.2), channel_id=1, source_target_pairs={{0,32},{32,0},{64,96},{96,64},{128,160},{160,128},{192,224},{224,1... | collective-permute-start | bytes 1105928 | tf_op jit(solution)/shard_map/ppermute | solution.py:135
  45.7 15.3 %collective-permute-start.6 = (bf16[4,40,1152]{2,1,0:T(8,128)(2,1)S(1)}, bf16[4,40,1152]{2,1,0:T(8,128)(2,1)S(1)}, u32[]{:S(2)}, u32[]{:S(2)}) collective-permute-start(bf16[4,40,1152]{2,1,0:T(8,128)(2,1)S(1)} %dynamic-slice_bitcast_fusion), channel_id=1, source_target_pairs={{0,32},{32,0},{64,96},{96,64},{128,160},{160,128},{192,224},{224,1... | collective-permute-start | bytes 1105928 | tf_op jit(solution)/shard_map/ppermute | solution.py:135
  54.5 10.2 %collective-permute-start.4 = (bf16[320,256]{1,0:T(8,128)(2,1)S(1)}, bf16[320,256]{1,0:T(8,128)(2,1)S(1)}, u32[]{:S(2)}, u32[]{:S(2)}) collective-permute-start(bf16[320,256]{1,0:T(8,128)(2,1)S(1)} %convolution_convert_fusion), channel_id=1, source_target_pairs={{0,16},{16,0},{1,17},{17,1},{2,18},{18,2},{3,19},{19,3},{4,20},{20... | collective-permute-start | bytes 491528 | tf_op jit(solution)/shard_map/ppermute | solution.py:127
  61.2 13.0 %collective-permute-start.7 = (bf16[2,40,1152]{2,1,0:T(8,128)(2,1)S(1)}, bf16[2,40,1152]{2,1,0:T(8,128)(2,1)S(1)}, u32[]{:S(2)}, u32[]{:S(2)}) collective-permute-start(bf16[2,40,1152]{2,1,0:T(8,128)(2,1)S(1)} %dynamic-slice_bitcast_fusion.1), channel_id=1, source_target_pairs={{0,64},{32,96},{64,0},{96,32},{128,192},{160,224},{192,128},{224,1... | collective-permute-start | bytes 552968 | tf_op jit(solution)/shard_map/ppermute | solution.py:135
  66.2 21.1 %all-to-all-start.1 = ((bf16[16,40,256]{2,1,0:T(8,128)(2,1)}), bf16[16,40,256]{2,1,0:T(8,128)(2,1)S(1)}, u32[]{:S(2)}, u32[]{:S(2)}) async-start(bf16[16,40,256]{2,1,0:T(8,128)(2,1)} %shard_map.94), calls=%async_computation.1 | async-start | bytes 655360 | tf_op jit(solution)/shard_map/all_to_all | solution.py:131
  74.3 9.9 %collective-permute-start.8 = (bf16[1,40,1152]{2,1,0:T(8,128)(2,1)S(1)}, bf16[1,40,1152]{2,1,0:T(8,128)(2,1)S(1)}, u32[]{:S(2)}, u32[]{:S(2)}) collective-permute-start(bf16[1,40,1152]{2,1,0:T(8,128)(2,1)S(1)} %get-tuple-element.28), channel_id=1, source_target_pairs={{0,128},{32,160},{64,192},{96,224},{128,0},{160,32},{192,64},{224,... | collective-permute-start | bytes 276488 | tf_op jit(solution)/shard_map/ppermute | solution.py:135
  88.0 19.2 %all-to-all-start.2 = ((bf16[32,24,128]{2,1,0:T(8,128)(2,1)}), bf16[32,24,128]{2,1,0:T(8,128)(2,1)S(1)}, u32[]{:S(2)}, u32[]{:S(2)}) async-start(bf16[32,24,128]{2,1,0:T(8,128)(2,1)} %pad_maximum_fusion.4), calls=%async_computation.2 | async-start | bytes 393216 | tf_op jit(solution)/shard_map/all_to_all | solution.py:131
